TPU v7x, 32 devices: a whole 2x2x4 slice. The times are simulated.
32 devices in a mesh: ctx: 8 (over z, y), fsdp: 4 (over x, core).
Axes of the slice: x: 2, y: 2, z: 4, core: 2. Of those that a mesh axis runs over, the one named last changes fastest.
Arguments:
- tokens: bfloat16 [4, 16, 128, 1024], P('fsdp', None, 'ctx'), may hold values from -6 to 6
- lengths: int32 [4, 3], P('fsdp'), may hold values from 512 to 1024, as said below
- packing: int32 [4, 3], P('fsdp'), may hold values from 0 to 2, each once within a row
- query_w: bfloat16 [1024, 1024], P('fsdp'), may hold values from -0.1875 to 0.1875
- query_b: float32 [1024], replicated, may hold values from -3 to 3
- key_w: bfloat16 [1024, 1024], P('fsdp'), may hold values from -0.1875 to 0.1875
- value_w: bfloat16 [1024, 1024], P('fsdp'), may hold values from -0.1875 to 0.1875
- value_b: float32 [1024], replicated, may hold values from -3 to 3
- output_w: bfloat16 [1024, 1024], P('fsdp'), may hold values from -3 to 3
- output_b: float32 [1024], replicated, may hold values from -3 to 3
- attn_gain: float32 [1024], replicated, may hold values from 0.5 to 1.5
- attn_shift: float32 [1024], replicated, may hold values from -2 to 2
- expand_w: bfloat16 [1024, 4096], P('fsdp'), may hold values from -0.1875 to 0.1875
- expand_b: float32 [4096], replicated, may hold values from -3 to 3
- reduce_w: bfloat16 [4096, 1024], P('fsdp'), may hold values from -0.09375 to 0.09375
- reduce_b: float32 [1024], replicated, may hold values from -3 to 3
- ffn_gain: float32 [1024], replicated, may hold values from 0.5 to 1.5
- ffn_shift: float32 [1024], replicated, may hold values from -2 to 2
- cotangent: bfloat16 [4, 16, 128, 1024], P('fsdp', None, 'ctx'), may hold values from -6 to 6
Outputs:
- layer_out: bfloat16 [4, 16, 128, 1024], P('fsdp', None, 'ctx')
- grad_tokens: float32 [4, 16, 128, 1024], P('fsdp', None, 'ctx')
- grad_query_w: float32 [1024, 1024], P('fsdp')
- grad_query_b: float32 [1024], replicated
- grad_key_w: float32 [1024, 1024], P('fsdp')
- grad_value_w: float32 [1024, 1024], P('fsdp')
- grad_value_b: float32 [1024], replicated
- grad_output_w: float32 [1024, 1024], P('fsdp')
- grad_output_b: float32 [1024], replicated
- grad_attn_gain: float32 [1024], replicated
- grad_attn_shift: float32 [1024], replicated
- grad_expand_w: float32 [1024, 4096], P('fsdp')
- grad_expand_b: float32 [4096], replicated
- grad_reduce_w: float32 [4096, 1024], P('fsdp')
- grad_reduce_b: float32 [1024], replicated
- grad_ffn_gain: float32 [1024], replicated
- grad_ffn_shift: float32 [1024], replicated
Inputs may be any that keep to these rules, and one draw needn't show every extreme that they name: Each row's 3 lengths sum to 2048. Each row of packing names every sequence once.
All inputs are finite; a program needn't handle non-finite values.
Results may differ from a plain program's by a relative error of at most 0.02.
Values may be sent and summed in bfloat16 or wider, within the bound.
A program may use at most 192 MiB of HBM per device.

v0:
```python
import jax
import jax.numpy as jnp
from jax import lax
from jax.sharding import PartitionSpec as P

H = 16
HD = 64


def from_behind(block, axis, distance):
    devices = range(lax.axis_size(axis))
    route = [((i - distance) % len(devices), i) for i in devices]
    return lax.ppermute(block, axis, route)


def dense(left, right):
    return jnp.dot(left, right, preferred_element_type=jnp.float32)


def dense_back(left, right):
    return lax.dot_general(
        left, right, (((1,), (1,)), ((), ())), preferred_element_type=jnp.float32
    )


def norm_fwd(hidden, gain, shift):
    mean_row = jnp.mean(hidden, axis=-1, keepdims=True)
    centred = hidden - mean_row
    variance = jnp.mean(centred * centred, axis=-1, keepdims=True)
    inv_std = lax.rsqrt(variance + 1e-05)
    x_hat = centred * inv_std
    return (x_hat * gain + shift, x_hat, inv_std)


def norm_back(incoming, x_hat, inv_std, gain):
    scaled = incoming * gain
    grad_in = inv_std * (
        scaled
        - jnp.mean(scaled, axis=-1, keepdims=True)
        - x_hat * jnp.mean(scaled * x_hat, axis=-1, keepdims=True)
    )
    return (grad_in, jnp.sum(incoming * x_hat, axis=0), jnp.sum(incoming, axis=0))


def gelu_slope(pre_act):
    return (
        0.5 * (1.0 + lax.erf(pre_act * 0.7071067811865476))
        + pre_act * jnp.exp(-0.5 * pre_act * pre_act) * 0.3989422804014327
    )


def online_update(running, query_heads, query_seg, key_rows, value_rows, key_seg):
    accum, run_max, run_sum = running
    rows_here = key_rows.shape[0]
    scores = 0.125 * jnp.einsum(
        "qhd,khd->hqk",
        query_heads,
        key_rows.reshape(rows_here, H, HD),
        preferred_element_type=jnp.float32,
    )
    same_seg = (query_seg[:, None] == key_seg[None, :])[None]
    masked = jnp.where(same_seg, scores, -1e30)
    new_max = jnp.maximum(run_max, jnp.max(masked, axis=-1))
    scale_old = jnp.exp(run_max - new_max)
    exp_scores = jnp.where(same_seg, jnp.exp(masked - new_max[:, :, None]), 0.0)
    run_sum = run_sum * scale_old + jnp.sum(exp_scores, axis=-1)
    update = jnp.einsum(
        "hqk,khd->qhd",
        exp_scores.astype(jnp.bfloat16),
        value_rows.reshape(rows_here, H, HD),
        preferred_element_type=jnp.float32,
    )
    accum = accum * scale_old.T[:, :, None] + update
    return (accum, new_max, run_sum)


def pair_grads(query_rows, grad_rows, log_sum, delta_row, query_seg, key_rows, value_rows, key_seg):
    q_heads = query_rows.reshape(-1, H, HD)
    g_heads = grad_rows.reshape(-1, H, HD)
    k_heads = key_rows.reshape(-1, H, HD)
    v_heads = value_rows.reshape(-1, H, HD)
    scores = 0.125 * jnp.einsum(
        "qhd,khd->hqk", q_heads, k_heads, preferred_element_type=jnp.float32
    )
    same_seg = (query_seg[:, None] == key_seg[None, :])[None]
    probs = jnp.where(
        same_seg, jnp.exp(jnp.where(same_seg, scores, -1e30) - log_sum[:, :, None]), 0.0
    )
    grad_prob = jnp.einsum("qhd,khd->hqk", g_heads, v_heads, preferred_element_type=jnp.float32)
    grad_score = (probs * (grad_prob - delta_row[:, :, None])).astype(jnp.bfloat16)
    grad_q = 0.125 * jnp.einsum(
        "hqk,khd->qhd", grad_score, k_heads, preferred_element_type=jnp.float32
    )
    grad_k = 0.125 * jnp.einsum(
        "hqk,qhd->khd", grad_score, q_heads, preferred_element_type=jnp.float32
    )
    grad_v = jnp.einsum(
        "hqk,qhd->khd", probs.astype(jnp.bfloat16), g_heads, preferred_element_type=jnp.float32
    )
    return (
        grad_q.reshape(query_rows.shape),
        grad_k.reshape(key_rows.shape),
        grad_v.reshape(key_rows.shape),
    )


def owner_rows(layer_in, layer_grad):
    return lax.psum_scatter(
        lax.dot_general(
            layer_in, layer_grad, (((0,), (0,)), ((), ())), preferred_element_type=jnp.float32
        ).astype(jnp.bfloat16),
        "fsdp",
        scatter_dimension=0,
        tiled=True,
    ).astype(jnp.float32)


def body(
    tokens,
    lengths,
    packing,
    query_w,
    query_b,
    key_w,
    value_w,
    value_b,
    output_w,
    output_b,
    attn_gain,
    attn_shift,
    expand_w,
    expand_b,
    reduce_w,
    reduce_b,
    ffn_gain,
    ffn_shift,
    cotangent,
):
    tok_shape = tokens.shape
    stripe = tok_shape[2]
    block_len = tok_shape[1] * tok_shape[2]
    model_width = tok_shape[3]
    n_ctx = lax.axis_size("ctx")
    ctx_index = lax.axis_index("ctx")
    seq_lens = lengths[0]
    slot_ids = packing[0]
    ordered = jnp.sum(
        jnp.where(
            slot_ids[:, None] == jnp.arange(seq_lens.shape[0], dtype=jnp.int32)[None, :],
            seq_lens[None, :],
            0,
        ),
        axis=1,
    )
    slots = jnp.arange(seq_lens.shape[0], dtype=jnp.int32)
    slot_ends = jnp.sum(jnp.where(slots[None, :] <= slots[:, None], ordered[None, :], 0), axis=1)
    gathered = jnp.arange(n_ctx * block_len, dtype=jnp.int32)
    owner_dev = gathered // block_len
    local_row = gathered % block_len
    position = local_row // stripe * (stripe * n_ctx) + owner_dev * stripe + local_row % stripe
    seg_all = jnp.sum((position[:, None] >= slot_ends[None, :]).astype(jnp.int32), axis=1)
    query_seg = lax.dynamic_slice_in_dim(seg_all, ctx_index * block_len, block_len)
    inputs = tokens.reshape(block_len, model_width)
    w_query, w_key, w_value, w_output, w_up, w_down = (
        lax.all_gather(query_w, "fsdp", axis=0, tiled=True),
        lax.all_gather(key_w, "fsdp", axis=0, tiled=True),
        lax.all_gather(value_w, "fsdp", axis=0, tiled=True),
        lax.all_gather(output_w, "fsdp", axis=0, tiled=True),
        lax.all_gather(expand_w, "fsdp", axis=0, tiled=True),
        lax.all_gather(reduce_w, "fsdp", axis=0, tiled=True),
    )
    queries = (dense(inputs, w_query) + query_b).astype(jnp.bfloat16)
    key_rows = dense(inputs, w_key).astype(jnp.bfloat16)
    values = (dense(inputs, w_value) + value_b).astype(jnp.bfloat16)
    query_heads = queries.reshape(block_len, H, HD)
    start_state = (
        jnp.zeros((block_len, H, HD), jnp.float32),
        jnp.full((H, block_len), -1e30, jnp.float32),
        jnp.zeros((H, block_len), jnp.float32),
    )
    key_piece = lax.all_gather(key_rows, "ctx", axis=0, tiled=True)
    value_piece = lax.all_gather(values, "ctx", axis=0, tiled=True)
    shards = key_piece.shape[0] // block_len

    def one_shard(index, inner):
        key_part = lax.dynamic_slice_in_dim(key_piece, index * block_len, block_len)
        value_part = lax.dynamic_slice_in_dim(value_piece, index * block_len, block_len)
        key_seg = lax.dynamic_slice_in_dim(seg_all, index * block_len, block_len)
        return online_update(inner, query_heads, query_seg, key_part, value_part, key_seg)

    accum, run_max, run_sum = lax.fori_loop(0, shards, one_shard, start_state)
    attended = (accum / run_sum.T[:, :, None]).reshape(block_len, model_width).astype(jnp.bfloat16)
    log_sum = run_max + jnp.log(run_sum)
    branch = dense(attended, w_output) + output_b
    normed, x_hat1, inv_std1 = norm_fwd(inputs.astype(jnp.float32) + branch, attn_gain, attn_shift)
    normed_low = normed.astype(jnp.bfloat16)
    pre_act = dense(normed_low, w_up) + expand_b
    hidden = jax.nn.gelu(pre_act, approximate=False).astype(jnp.bfloat16)
    ffn_out = dense(hidden, w_down) + reduce_b
    outputs, x_hat2, inv_std2 = norm_fwd(normed + ffn_out, ffn_gain, ffn_shift)
    layer_out = outputs.astype(jnp.bfloat16).reshape(tok_shape)
    upstream = cotangent.reshape(block_len, model_width).astype(jnp.float32)
    grad_mid2, grad_ffn_gain, grad_ffn_shift = norm_back(upstream, x_hat2, inv_std2, ffn_gain)
    grad_ffn = grad_mid2.astype(jnp.bfloat16)
    grad_reduce_b = jnp.sum(grad_ffn.astype(jnp.float32), axis=0)
    share_down = owner_rows(hidden, grad_ffn)
    grad_pre = (dense_back(grad_ffn, w_down) * gelu_slope(pre_act)).astype(jnp.bfloat16)
    grad_expand_b = jnp.sum(grad_pre.astype(jnp.float32), axis=0)
    share_up = owner_rows(normed_low, grad_pre)
    grad_normed = dense_back(grad_pre, w_up) + grad_mid2
    grad_mid1, grad_attn_gain, grad_attn_shift = norm_back(grad_normed, x_hat1, inv_std1, attn_gain)
    grad_branch = grad_mid1.astype(jnp.bfloat16)
    grad_output_b = jnp.sum(grad_branch.astype(jnp.float32), axis=0)
    share_out = owner_rows(attended, grad_branch)
    grad_att = dense_back(grad_branch, w_output).astype(jnp.bfloat16)
    delta_row = jnp.einsum(
        "qhd,qhd->hq",
        grad_att.astype(jnp.float32).reshape(block_len, H, HD),
        attended.astype(jnp.float32).reshape(block_len, H, HD),
    )
    zero_rows = jnp.zeros((block_len, model_width), jnp.float32)

    def key_step(step, state):
        visit_keys, visit_values, sum_k, sum_v, sum_q = state
        anchor = (ctx_index - step) % n_ctx
        key_seg = lax.dynamic_slice_in_dim(seg_all, anchor * block_len, block_len)
        part_q, part_k, part_v = pair_grads(
            queries, grad_att, log_sum, delta_row, query_seg, visit_keys, visit_values, key_seg
        )
        sum_q = sum_q + part_q
        visit_keys, visit_values = from_behind((visit_keys, visit_values), "ctx", 1)
        sum_k, sum_v = (
            from_behind((sum_k + part_k).astype(jnp.bfloat16), "ctx", 1).astype(jnp.float32),
            from_behind((sum_v + part_v).astype(jnp.bfloat16), "ctx", 1).astype(jnp.float32),
        )
        return (visit_keys, visit_values, sum_k, sum_v, sum_q)

    final = lax.fori_loop(0, n_ctx, key_step, (key_rows, values, zero_rows, zero_rows, zero_rows))
    sum_k, sum_v, sum_q = (final[2], final[3], final[4])
    grad_q = sum_q.astype(jnp.bfloat16)
    grad_k = sum_k.astype(jnp.bfloat16)
    grad_v = sum_v.astype(jnp.bfloat16)
    grad_query_b = jnp.sum(grad_q.astype(jnp.float32), axis=0)
    grad_value_b = jnp.sum(grad_v.astype(jnp.float32), axis=0)
    share_query = owner_rows(inputs, grad_q)
    share_key = owner_rows(inputs, grad_k)
    share_value = owner_rows(inputs, grad_v)
    grad_inputs = (
        dense_back(grad_q, w_query)
        + dense_back(grad_k, w_key)
        + dense_back(grad_v, w_value)
        + grad_mid1
    )
    share_query, share_key, share_value, share_out, share_up, share_down = lax.psum(
        (share_query, share_key, share_value, share_out, share_up, share_down), "ctx"
    )
    (
        grad_query_b,
        grad_value_b,
        grad_output_b,
        grad_attn_gain,
        grad_attn_shift,
        grad_expand_b,
        grad_reduce_b,
        grad_ffn_gain,
        grad_ffn_shift,
    ) = lax.psum(
        (
            grad_query_b,
            grad_value_b,
            grad_output_b,
            grad_attn_gain,
            grad_attn_shift,
            grad_expand_b,
            grad_reduce_b,
            grad_ffn_gain,
            grad_ffn_shift,
        ),
        ("ctx", "fsdp"),
    )
    return (
        layer_out,
        grad_inputs.reshape(tok_shape),
        share_query,
        grad_query_b,
        share_key,
        share_value,
        grad_value_b,
        share_out,
        grad_output_b,
        grad_attn_gain,
        grad_attn_shift,
        share_up,
        grad_expand_b,
        share_down,
        grad_reduce_b,
        grad_ffn_gain,
        grad_ffn_shift,
    )


def solution(mesh):
    return jax.shard_map(
        body,
        mesh=mesh,
        in_specs=(
            P("fsdp", None, "ctx", None),
            P("fsdp", None),
            P("fsdp", None),
            P("fsdp", None),
            P(),
            P("fsdp", None),
            P("fsdp", None),
            P(),
            P("fsdp", None),
            P(),
            P(),
            P(),
            P("fsdp", None),
            P(),
            P("fsdp", None),
            P(),
            P(),
            P(),
            P("fsdp", None, "ctx", None),
        ),
        out_specs=(
            P("fsdp", None, "ctx", None),
            P("fsdp", None, "ctx", None),
            P("fsdp", None),
            P(),
            P("fsdp", None),
            P("fsdp", None),
            P(),
            P("fsdp", None),
            P(),
            P(),
            P(),
            P("fsdp", None),
            P(),
            P("fsdp", None),
            P(),
            P(),
            P(),
        ),
        check_vma=False,
    )
```

profile of v0, /device:TPU:0, one launch (start us, length us, event | category | flops | bytes accessed | tf_op | source)
XLA Modules:
  0.0 1579.9 jit_solution(7767871707761352350)
XLA Ops:
  9.5 25.4 %all-gather.9.cloned.1.call-done = bf16[1024,1024]{1,0:T(8,128)(2,1)} async-done(((bf16[256,1024]{1,0:T(8,128)(2,1)}), bf16[1024,1024]{1,0:T(8,128)(2,1)}) %all-gather.9.cloned.1.call-update) | async-done | bytes 2097168 | tf_op jit(solution)/shard_map/all_gather | solution.py:166
  34.9 3.3 convolution_convert_fusion.4
  38.3 20.8 %all-gather.15.cloned.1.call-done = bf16[1024,1024]{1,0:T(8,128)(2,1)} async-done(((bf16[256,1024]{1,0:T(8,128)(2,1)}), bf16[1024,1024]{1,0:T(8,128)(2,1)}) %all-gather.15.cloned.1.call-update) | async-done | bytes 2097168 | tf_op jit(solution)/shard_map/all_gather | solution.py:167
  59.1 3.1 fusion.45
  67.9 15.4 all-gather.13.cloned.1.call-done
  85.8 73.5 %all-gather.11.cloned.1.call-done = bf16[2048,1024]{1,0:T(8,128)(2,1)} async-done(((bf16[256,1024]{1,0:T(8,128)(2,1)}), bf16[2048,1024]{1,0:T(8,128)(2,1)}) %all-gather.11.cloned.1.call-update) | async-done | bytes 4194320 | tf_op jit(solution)/shard_map/all_gather | solution.py:181
  159.3 74.2 %all-gather.17.cloned.1.call-done = bf16[2048,1024]{1,0:T(8,128)(2,1)} async-done(((bf16[256,1024]{1,0:T(8,128)(2,1)}), bf16[2048,1024]{1,0:T(8,128)(2,1)}) %all-gather.17.cloned.1.call-update) | async-done | bytes 4194320 | tf_op jit(solution)/shard_map/all_gather | solution.py:182
  233.6 103.5 %while.42 = (s32[]{:T(128)}, f32[256,16,64]{0,2,1:T(8,128)}, f32[16,256]{1,0:T(8,128)S(1)}, f32[16,256]{1,0:T(8,128)S(1)}, s32[256]{0:T(256)S(1)}, /*index=5*/s3...) while((s32[]{:T(128)}, f32[256,16,64]{0,2,1:T(8,128)}, ...), condition=%wide.region_6.7_spmd.clone, body=%wide.region_3.6_spmd.clone.sunk | while | flops 282943488 | bytes 20975804 | solution.py:191
  238.1 3.4 fusion.156
  241.8 4.3 fusion.155
  250.6 3.2 fusion.156
  254.1 4.6 fusion.155
  263.2 3.8 fusion.156
  267.2 5.8 fusion.155
  277.6 3.2 fusion.156
  281.0 4.7 fusion.155
  290.2 3.2 fusion.156
  293.6 4.6 fusion.155
  302.8 3.3 fusion.156
  306.3 4.6 fusion.155
  315.4 3.2 fusion.156
  318.8 4.6 fusion.155
  325.3 3.1 fusion.153
  328.4 3.9 fusion.156
  332.5 4.6 fusion.155
  341.5 15.8 fusion.29
  357.3 18.4 %all-gather.23.cloned.1.call-done = bf16[4096,1024]{1,0:T(8,128)(2,1)} async-done(((bf16[1024,1024]{1,0:T(8,128)(2,1)}), bf16[4096,1024]{1,0:T(8,128)(2,1)}) %all-gather.23.cloned.1.call-update) | async-done | bytes 8388624 | tf_op jit(solution)/shard_map/all_gather | solution.py:170
  375.6 6.6 fusion.88
  384.5 4.2 convert_reduce_fusion
  394.0 406.6 %while.43 = (s32[]{:T(128)}, bf16[256,1024]{0,1:T(8,128)(2,1)}, bf16[256,1024]{0,1:T(8,128)(2,1)}, f32[256,1024]{0,1:T(8,128)}, f32[256,1024]{0,1:T(8,128)}, /*i...) while((s32[]{:T(128)}, bf16[256,1024]{0,1:T(8,128)(2,1)}, ...), condition=%wide.region_16.17_spmd.clone, body=%wide.region_15.16_spmd.clone.sunk | while | flops 686882816 | bytes 68932264 | solution.py:238
  401.2 3.1 multiply_convert_fusion.2
  414.1 21.3 %collective-permute-done.2 = bf16[256,1024]{0,1:T(8,128)(2,1)} collective-permute-done((bf16[256,1024]{0,1:T(8,128)(2,1)}, bf16[256,1024]{0,1:T(8,128)(2,1)}, u32[]{:S(2)}, u32[]{:S(2)}) %collective-permute-start.2) | collective-permute-done | bytes 524320 | tf_op jit(solution)/shard_map/while/body/eval_jaxpr/ppermute | solution.py:13
  437.5 8.5 collective-permute-done.3
  453.3 3.1 multiply_convert_fusion.2
  466.3 23.2 %collective-permute-done.2 = bf16[256,1024]{0,1:T(8,128)(2,1)} collective-permute-done((bf16[256,1024]{0,1:T(8,128)(2,1)}, bf16[256,1024]{0,1:T(8,128)(2,1)}, u32[]{:S(2)}, u32[]{:S(2)}) %collective-permute-start.2) | collective-permute-done | bytes 524320 | tf_op jit(solution)/shard_map/while/body/eval_jaxpr/ppermute | solution.py:13
  491.6 7.5 collective-permute-done.3
  505.3 3.1 multiply_convert_fusion.2
  517.6 25.0 %collective-permute-done.2 = bf16[256,1024]{0,1:T(8,128)(2,1)} collective-permute-done((bf16[256,1024]{0,1:T(8,128)(2,1)}, bf16[256,1024]{0,1:T(8,128)(2,1)}, u32[]{:S(2)}, u32[]{:S(2)}) %collective-permute-start.2) | collective-permute-done | bytes 524320 | tf_op jit(solution)/shard_map/while/body/eval_jaxpr/ppermute | solution.py:13
  544.7 6.6 collective-permute-done.3
  557.5 3.1 multiply_convert_fusion.2
  568.0 26.8 %collective-permute-done.2 = bf16[256,1024]{0,1:T(8,128)(2,1)} collective-permute-done((bf16[256,1024]{0,1:T(8,128)(2,1)}, bf16[256,1024]{0,1:T(8,128)(2,1)}, u32[]{:S(2)}, u32[]{:S(2)}) %collective-permute-start.2) | collective-permute-done | bytes 524320 | tf_op jit(solution)/shard_map/while/body/eval_jaxpr/ppermute | solution.py:13
  596.9 5.7 collective-permute-done.3
  608.8 3.1 multiply_convert_fusion.2
  618.9 27.2 %collective-permute-done.2 = bf16[256,1024]{0,1:T(8,128)(2,1)} collective-permute-done((bf16[256,1024]{0,1:T(8,128)(2,1)}, bf16[256,1024]{0,1:T(8,128)(2,1)}, u32[]{:S(2)}, u32[]{:S(2)}) %collective-permute-start.2) | collective-permute-done | bytes 524320 | tf_op jit(solution)/shard_map/while/body/eval_jaxpr/ppermute | solution.py:13
  648.2 4.8 collective-permute-done.3
  659.1 3.1 multiply_convert_fusion.2
  669.2 27.2 %collective-permute-done.2 = bf16[256,1024]{0,1:T(8,128)(2,1)} collective-permute-done((bf16[256,1024]{0,1:T(8,128)(2,1)}, bf16[256,1024]{0,1:T(8,128)(2,1)}, u32[]{:S(2)}, u32[]{:S(2)}) %collective-permute-start.2) | collective-permute-done | bytes 524320 | tf_op jit(solution)/shard_map/while/body/eval_jaxpr/ppermute | solution.py:13
  698.5 3.8 collective-permute-done.3
  708.6 3.1 multiply_convert_fusion.2
  718.6 26.6 %collective-permute-done.2 = bf16[256,1024]{0,1:T(8,128)(2,1)} collective-permute-done((bf16[256,1024]{0,1:T(8,128)(2,1)}, bf16[256,1024]{0,1:T(8,128)(2,1)}, u32[]{:S(2)}, u32[]{:S(2)}) %collective-permute-start.2) | collective-permute-done | bytes 524320 | tf_op jit(solution)/shard_map/while/body/eval_jaxpr/ppermute | solution.py:13
  747.3 3.5 collective-permute-done.3
  757.1 3.1 multiply_convert_fusion.2
  767.1 25.7 %collective-permute-done.2 = bf16[256,1024]{0,1:T(8,128)(2,1)} collective-permute-done((bf16[256,1024]{0,1:T(8,128)(2,1)}, bf16[256,1024]{0,1:T(8,128)(2,1)}, u32[]{:S(2)}, u32[]{:S(2)}) %collective-permute-start.2) | collective-permute-done | bytes 524320 | tf_op jit(solution)/shard_map/while/body/eval_jaxpr/ppermute | solution.py:13
  794.9 3.5 collective-permute-done.3
  800.6 3.5 convert_bitcast_fusion.2
  808.5 3.6 convolution_convert_fusion.2
  812.2 7.3 convolution_convert_fusion.1
  820.8 7.2 convolution_convert_fusion
  829.4 38.5 %all-reduce = (f32[1024]{0:T(1024)}, f32[1024]{0:T(1024)}, f32[1024]{0:T(1024)}, f32[1024]{0:T(1024)}, f32[1024]{0:T(1024)}, /*index=5*/f32[4096]{0:T(1024)}, f32[1024]{0:T(1024)}, f32[1024]{0:T(1024)}, f32[1024]{0:T(1024)}) all-reduce(f32[1024]{0:T(1024)S(1)} %convert_reduce_fusion.5, ...), channel_id=1, replica_groups=mesh['ctx'=8,'fsdp'=4] {'ctx','fsdp'}, use_global_device_ids=true, to_apply=%region_20.21 | all-reduce | flops 12288 | bytes 98304 | tf_op jit(solution)/shard_map/psum | solution.py:267
  874.6 26.8 %reduce-scatter.11.cloned.1.call-done = bf16[256,1024]{0,1:T(8,128)(2,1)} async-done(((bf16[1024,1024]{0,1:T(8,128)(2,1)}), bf16[256,1024]{0,1:T(8,128)(2,1)}) %reduce-scatter.11.cloned.1.call-update) | async-done | bytes 524304 | tf_op jit(solution)/shard_map/reduce_scatter | solution.py:108
  901.4 34.0 %reduce-scatter.13.cloned.1.call-done = bf16[256,1024]{1,0:T(8,128)(2,1)} async-done(((bf16[1024,1024]{1,0:T(8,128)(2,1)}), bf16[256,1024]{1,0:T(8,128)(2,1)}) %reduce-scatter.13.cloned.1.call-update) | async-done | bytes 524304 | tf_op jit(solution)/shard_map/reduce_scatter | solution.py:108
  935.4 74.3 %reduce-scatter.15.cloned.1.call-done = bf16[256,4096]{1,0:T(8,128)(2,1)} async-done(((bf16[1024,4096]{1,0:T(8,128)(2,1)}), bf16[256,4096]{1,0:T(8,128)(2,1)}) %reduce-scatter.15.cloned.1.call-update) | async-done | bytes 2097168 | tf_op jit(solution)/shard_map/reduce_scatter | solution.py:108
  1009.7 74.4 %reduce-scatter.17.cloned.1.call-done = bf16[1024,1024]{1,0:T(8,128)(2,1)} async-done(((bf16[4096,1024]{1,0:T(8,128)(2,1)}), bf16[1024,1024]{1,0:T(8,128)(2,1)}) %reduce-scatter.17.cloned.1.call-update) | async-done | bytes 2097168 | tf_op jit(solution)/shard_map/reduce_scatter | solution.py:108
  1084.1 485.2 %all-reduce.3 = (f32[256,1024]{0,1:T(8,128)S(1)}, f32[256,1024]{0,1:T(8,128)S(1)}, f32[256,1024]{0,1:T(8,128)S(1)}, f32[256,1024]{1,0:T(8,128)}, f32[256,4096]{1,0:T(8,128)}, /*index=5*/f32[1024,1024]{1,0:T(8,128)}) all-reduce(bf16[256,1024]{0,1:T(8,128)(2,1)} %reduce-scatter.7.cloned.1.call-done, ...), channel_id=1, replica_groups=mesh['ctx'=8,'fsdp'=4] {'ctx'}, use_global_device_ids=true, to_apply=%region_18.19 | all-reduce | flops 3145728 | bytes 18874368 | tf_op jit(solution)/shard_map/psum | solution.py:254
  (471 shorter events, 208.3 us)
Async XLA Ops:
  7.2 51.9 %copy-start.11 = (bf16[1,16,16,1024]{3,2,1,0:T(8,128)(2,1)S(1)}, bf16[1,16,16,1024]{3,2,1,0:T(8,128)(2,1)}, u32[]{:S(2)}) copy-start(bf16[1,16,16,1024]{3,2,1,0:T(8,128)(2,1)} %param.23) | copy-start | bytes 1572868
  7.2 51.9 %copy-start.32 = (f32[1024]{0:T(1024)S(1)}, f32[1024]{0:T(1024)}, u32[]{:S(2)}) copy-start(f32[1024]{0:T(1024)} %param.30) | copy-start | bytes 12292
  7.2 27.7 %all-gather.9.cloned.1.call-start = ((), (), s32[]{:S(2)}) async-start(), calls=%async_computation.6 | async-start | bytes 2621440 | tf_op jit(solution)/shard_map/all_gather | solution.py:166
  7.9 51.2 %all-gather.15.cloned.1.call-start = ((), (), s32[]{:S(2)}) async-start(), calls=%async_computation.9 | async-start | bytes 2621440 | tf_op jit(solution)/shard_map/all_gather | solution.py:167
  8.7 74.6 %all-gather.13.cloned.1.call-start = ((), (), s32[]{:S(2)}) async-start(), calls=%async_computation.8 | async-start | bytes 2621440 | tf_op jit(solution)/shard_map/all_gather | solution.py:165
  9.4 149.9 %all-gather.11.cloned.1.call-start = ((), (), s32[]{:S(2)}) async-start(), calls=%async_computation.7 | async-start | bytes 4718592 | tf_op jit(solution)/shard_map/all_gather | solution.py:181
  38.3 195.3 %all-gather.17.cloned.1.call-start = ((), (), s32[]{:S(2)}) async-start(), calls=%async_computation.10 | async-start | bytes 4718592 | tf_op jit(solution)/shard_map/all_gather | solution.py:182
  62.2 276.3 %all-gather.19.cloned.1.call-start = ((), (), s32[]{:S(2)}) async-start(), calls=%async_computation.11 | async-start | bytes 2621440 | tf_op jit(solution)/shard_map/all_gather | solution.py:168
  62.8 278.6 %all-gather.21.cloned.1.call-start = ((), (), s32[]{:S(2)}) async-start(), calls=%async_computation.12 | async-start | bytes 10485760 | tf_op jit(solution)/shard_map/all_gather | solution.py:169
  63.6 312.1 %all-gather.23.cloned.1.call-start = ((), (), s32[]{:S(2)}) async-start(), calls=%async_computation.13 | async-start | bytes 10485760 | tf_op jit(solution)/shard_map/all_gather | solution.py:170
  64.3 810.3 %reduce-scatter.7.cloned.1.call-start = ((), (), s32[]{:S(2)}) async-start(), calls=%async_computation.14 | async-start | bytes 2621440 | tf_op jit(solution)/shard_map/reduce_scatter | solution.py:108
  233.6 105.0 %copy-start.28 = (f32[1024]{0:T(1024)S(1)}, f32[1024]{0:T(1024)}, u32[]{:S(2)}) copy-start(f32[1024]{0:T(1024)} %param.32) | copy-start | bytes 12292
  341.1 50.3 %copy-start.7 = (f32[256,1024]{1,0:T(8,128)}, f32[256,1024]{1,0:T(8,128)S(1)}, u32[]{:S(2)}) copy-start(f32[256,1024]{1,0:T(8,128)S(1)} %get-tuple-element.758) | copy-start | bytes 3145732
  341.4 34.2 %copy-start.34 = (f32[1024]{0:T(1024)S(1)}, f32[1024]{0:T(1024)}, u32[]{:S(2)}) copy-start(f32[1024]{0:T(1024)} %param.38) | copy-start | bytes 12292
  395.4 52.7 %collective-permute-start = (bf16[256,1024]{0,1:T(8,128)(2,1)S(1)}, bf16[256,1024]{0,1:T(8,128)(2,1)}, u32[]{:S(2)}, u32[]{:S(2)}) collective-permute-start(bf16[256,1024]{0,1:T(8,128)(2,1)S(1)} %copy.106), channel_id=1, source_target_pairs={{28,0},{0,4},{4,8},{8,12},{12,16},{16,20},{20,24},{24,28},{29,1},{... | collective-permute-start | bytes 1572872 | tf_op jit(solution)/shard_map/while/body/eval_jaxpr/ppermute | solution.py:13
  398.7 49.3 %collective-permute-start.1 = (bf16[256,1024]{0,1:T(8,128)(2,1)}, bf16[256,1024]{0,1:T(8,128)(2,1)}, u32[]{:S(2)}, u32[]{:S(2)}) collective-permute-start(bf16[256,1024]{0,1:T(8,128)(2,1)} %copy.107), channel_id=1, source_target_pairs={{28,0},{0,4},{4,8},{8,12},{12,16},{16,20},{20,24},{24,28},{29,1},{... | collective-permute-start | bytes 1572872 | tf_op jit(solution)/shard_map/while/body/eval_jaxpr/ppermute | solution.py:13
  406.4 29.0 %collective-permute-start.2 = (bf16[256,1024]{0,1:T(8,128)(2,1)}, bf16[256,1024]{0,1:T(8,128)(2,1)}, u32[]{:S(2)}, u32[]{:S(2)}) collective-permute-start(bf16[256,1024]{0,1:T(8,128)(2,1)} %fusion.169), channel_id=1, source_target_pairs={{28,0},{0,4},{4,8},{8,12},{12,16},{16,20},{20,24},{24,28},{29,1},{... | collective-permute-start | bytes 1572872 | tf_op jit(solution)/shard_map/while/body/eval_jaxpr/ppermute | solution.py:13
  411.2 34.8 %collective-permute-start.3 = (bf16[256,1024]{0,1:T(8,128)(2,1)}, bf16[256,1024]{0,1:T(8,128)(2,1)}, u32[]{:S(2)}, u32[]{:S(2)}) collective-permute-start(bf16[256,1024]{0,1:T(8,128)(2,1)} %fusion.171), channel_id=1, source_target_pairs={{28,0},{0,4},{4,8},{8,12},{12,16},{16,20},{20,24},{24,28},{29,1},{... | collective-permute-start | bytes 1572872 | tf_op jit(solution)/shard_map/while/body/eval_jaxpr/ppermute | solution.py:13
  413.4 34.7 %copy-start.22 = (bf16[256,1024]{0,1:T(8,128)(2,1)S(1)}, bf16[256,1024]{0,1:T(8,128)(2,1)}, u32[]{:S(2)}) copy-start(bf16[256,1024]{0,1:T(8,128)(2,1)} %copy-done.21) | copy-start | bytes 1572868 | tf_op jit(solution)/shard_map/while
  449.3 51.9 %collective-permute-start = (bf16[256,1024]{0,1:T(8,128)(2,1)S(1)}, bf16[256,1024]{0,1:T(8,128)(2,1)}, u32[]{:S(2)}, u32[]{:S(2)}) collective-permute-start(bf16[256,1024]{0,1:T(8,128)(2,1)S(1)} %copy.106), channel_id=1, source_target_pairs={{28,0},{0,4},{4,8},{8,12},{12,16},{16,20},{20,24},{24,28},{29,1},{... | collective-permute-start | bytes 1572872 | tf_op jit(solution)/shard_map/while/body/eval_jaxpr/ppermute | solution.py:13
  451.2 50.0 %collective-permute-start.1 = (bf16[256,1024]{0,1:T(8,128)(2,1)}, bf16[256,1024]{0,1:T(8,128)(2,1)}, u32[]{:S(2)}, u32[]{:S(2)}) collective-permute-start(bf16[256,1024]{0,1:T(8,128)(2,1)} %copy.107), channel_id=1, source_target_pairs={{28,0},{0,4},{4,8},{8,12},{12,16},{16,20},{20,24},{24,28},{29,1},{... | collective-permute-start | bytes 1572872 | tf_op jit(solution)/shard_map/while/body/eval_jaxpr/ppermute | solution.py:13
  458.6 30.9 %collective-permute-start.2 = (bf16[256,1024]{0,1:T(8,128)(2,1)}, bf16[256,1024]{0,1:T(8,128)(2,1)}, u32[]{:S(2)}, u32[]{:S(2)}) collective-permute-start(bf16[256,1024]{0,1:T(8,128)(2,1)} %fusion.169), channel_id=1, source_target_pairs={{28,0},{0,4},{4,8},{8,12},{12,16},{16,20},{20,24},{24,28},{29,1},{... | collective-permute-start | bytes 1572872 | tf_op jit(solution)/shard_map/while/body/eval_jaxpr/ppermute | solution.py:13
  462.5 36.7 %collective-permute-start.3 = (bf16[256,1024]{0,1:T(8,128)(2,1)}, bf16[256,1024]{0,1:T(8,128)(2,1)}, u32[]{:S(2)}, u32[]{:S(2)}) collective-permute-start(bf16[256,1024]{0,1:T(8,128)(2,1)} %fusion.171), channel_id=1, source_target_pairs={{28,0},{0,4},{4,8},{8,12},{12,16},{16,20},{20,24},{24,28},{29,1},{... | collective-permute-start | bytes 1572872 | tf_op jit(solution)/shard_map/while/body/eval_jaxpr/ppermute | solution.py:13
  465.6 35.6 %copy-start.22 = (bf16[256,1024]{0,1:T(8,128)(2,1)S(1)}, bf16[256,1024]{0,1:T(8,128)(2,1)}, u32[]{:S(2)}) copy-start(bf16[256,1024]{0,1:T(8,128)(2,1)} %copy-done.21) | copy-start | bytes 1572868 | tf_op jit(solution)/shard_map/while
  466.2 35.0 %copy-start.3 = (f32[256,1024]{0,1:T(8,128)}, f32[256,1024]{0,1:T(8,128)S(1)}, u32[]{:S(2)}) copy-start(f32[256,1024]{0,1:T(8,128)S(1)} %bitcast_add_fusion.4) | copy-start | bytes 3145732 | tf_op jit(solution)/shard_map/while
  502.5 50.9 %collective-permute-start = (bf16[256,1024]{0,1:T(8,128)(2,1)S(1)}, bf16[256,1024]{0,1:T(8,128)(2,1)}, u32[]{:S(2)}, u32[]{:S(2)}) collective-permute-start(bf16[256,1024]{0,1:T(8,128)(2,1)S(1)} %copy.106), channel_id=1, source_target_pairs={{28,0},{0,4},{4,8},{8,12},{12,16},{16,20},{20,24},{24,28},{29,1},{... | collective-permute-start | bytes 1572872 | tf_op jit(solution)/shard_map/while/body/eval_jaxpr/ppermute | solution.py:13
  504.4 49.1 %collective-permute-start.1 = (bf16[256,1024]{0,1:T(8,128)(2,1)}, bf16[256,1024]{0,1:T(8,128)(2,1)}, u32[]{:S(2)}, u32[]{:S(2)}) collective-permute-start(bf16[256,1024]{0,1:T(8,128)(2,1)} %copy.107), channel_id=1, source_target_pairs={{28,0},{0,4},{4,8},{8,12},{12,16},{16,20},{20,24},{24,28},{29,1},{... | collective-permute-start | bytes 1572872 | tf_op jit(solution)/shard_map/while/body/eval_jaxpr/ppermute | solution.py:13
  510.6 32.0 %collective-permute-start.2 = (bf16[256,1024]{0,1:T(8,128)(2,1)}, bf16[256,1024]{0,1:T(8,128)(2,1)}, u32[]{:S(2)}, u32[]{:S(2)}) collective-permute-start(bf16[256,1024]{0,1:T(8,128)(2,1)} %fusion.169), channel_id=1, source_target_pairs={{28,0},{0,4},{4,8},{8,12},{12,16},{16,20},{20,24},{24,28},{29,1},{... | collective-permute-start | bytes 1572872 | tf_op jit(solution)/shard_map/while/body/eval_jaxpr/ppermute | solution.py:13
  513.9 37.4 %collective-permute-start.3 = (bf16[256,1024]{0,1:T(8,128)(2,1)}, bf16[256,1024]{0,1:T(8,128)(2,1)}, u32[]{:S(2)}, u32[]{:S(2)}) collective-permute-start(bf16[256,1024]{0,1:T(8,128)(2,1)} %fusion.171), channel_id=1, source_target_pairs={{28,0},{0,4},{4,8},{8,12},{12,16},{16,20},{20,24},{24,28},{29,1},{... | collective-permute-start | bytes 1572872 | tf_op jit(solution)/shard_map/while/body/eval_jaxpr/ppermute | solution.py:13
  516.9 36.5 %copy-start.22 = (bf16[256,1024]{0,1:T(8,128)(2,1)S(1)}, bf16[256,1024]{0,1:T(8,128)(2,1)}, u32[]{:S(2)}) copy-start(bf16[256,1024]{0,1:T(8,128)(2,1)} %copy-done.21) | copy-start | bytes 1572868 | tf_op jit(solution)/shard_map/while
  517.6 35.8 %copy-start.3 = (f32[256,1024]{0,1:T(8,128)}, f32[256,1024]{0,1:T(8,128)S(1)}, u32[]{:S(2)}) copy-start(f32[256,1024]{0,1:T(8,128)S(1)} %bitcast_add_fusion.4) | copy-start | bytes 3145732 | tf_op jit(solution)/shard_map/while
  554.7 50.0 %collective-permute-start = (bf16[256,1024]{0,1:T(8,128)(2,1)S(1)}, bf16[256,1024]{0,1:T(8,128)(2,1)}, u32[]{:S(2)}, u32[]{:S(2)}) collective-permute-start(bf16[256,1024]{0,1:T(8,128)(2,1)S(1)} %copy.106), channel_id=1, source_target_pairs={{28,0},{0,4},{4,8},{8,12},{12,16},{16,20},{20,24},{24,28},{29,1},{... | collective-permute-start | bytes 1572872 | tf_op jit(solution)/shard_map/while/body/eval_jaxpr/ppermute | solution.py:13
  556.6 48.1 %collective-permute-start.1 = (bf16[256,1024]{0,1:T(8,128)(2,1)}, bf16[256,1024]{0,1:T(8,128)(2,1)}, u32[]{:S(2)}, u32[]{:S(2)}) collective-permute-start(bf16[256,1024]{0,1:T(8,128)(2,1)} %copy.107), channel_id=1, source_target_pairs={{28,0},{0,4},{4,8},{8,12},{12,16},{16,20},{20,24},{24,28},{29,1},{... | collective-permute-start | bytes 1572872 | tf_op jit(solution)/shard_map/while/body/eval_jaxpr/ppermute | solution.py:13
  562.8 32.0 %collective-permute-start.2 = (bf16[256,1024]{0,1:T(8,128)(2,1)}, bf16[256,1024]{0,1:T(8,128)(2,1)}, u32[]{:S(2)}, u32[]{:S(2)}) collective-permute-start(bf16[256,1024]{0,1:T(8,128)(2,1)} %fusion.169), channel_id=1, source_target_pairs={{28,0},{0,4},{4,8},{8,12},{12,16},{16,20},{20,24},{24,28},{29,1},{... | collective-permute-start | bytes 1572872 | tf_op jit(solution)/shard_map/while/body/eval_jaxpr/ppermute | solution.py:13
  566.1 36.5 %collective-permute-start.3 = (bf16[256,1024]{0,1:T(8,128)(2,1)}, bf16[256,1024]{0,1:T(8,128)(2,1)}, u32[]{:S(2)}, u32[]{:S(2)}) collective-permute-start(bf16[256,1024]{0,1:T(8,128)(2,1)} %fusion.171), channel_id=1, source_target_pairs={{28,0},{0,4},{4,8},{8,12},{12,16},{16,20},{20,24},{24,28},{29,1},{... | collective-permute-start | bytes 1572872 | tf_op jit(solution)/shard_map/while/body/eval_jaxpr/ppermute | solution.py:13
  567.3 37.4 %copy-start.22 = (bf16[256,1024]{0,1:T(8,128)(2,1)S(1)}, bf16[256,1024]{0,1:T(8,128)(2,1)}, u32[]{:S(2)}) copy-start(bf16[256,1024]{0,1:T(8,128)(2,1)} %copy-done.21) | copy-start | bytes 1572868 | tf_op jit(solution)/shard_map/while
  568.0 36.7 %copy-start.3 = (f32[256,1024]{0,1:T(8,128)}, f32[256,1024]{0,1:T(8,128)S(1)}, u32[]{:S(2)}) copy-start(f32[256,1024]{0,1:T(8,128)S(1)} %bitcast_add_fusion.4) | copy-start | bytes 3145732 | tf_op jit(solution)/shard_map/while
  606.0 49.1 %collective-permute-start = (bf16[256,1024]{0,1:T(8,128)(2,1)S(1)}, bf16[256,1024]{0,1:T(8,128)(2,1)}, u32[]{:S(2)}, u32[]{:S(2)}) collective-permute-start(bf16[256,1024]{0,1:T(8,128)(2,1)S(1)} %copy.106), channel_id=1, source_target_pairs={{28,0},{0,4},{4,8},{8,12},{12,16},{16,20},{20,24},{24,28},{29,1},{... | collective-permute-start | bytes 1572872 | tf_op jit(solution)/shard_map/while/body/eval_jaxpr/ppermute | solution.py:13
  607.8 47.2 %collective-permute-start.1 = (bf16[256,1024]{0,1:T(8,128)(2,1)}, bf16[256,1024]{0,1:T(8,128)(2,1)}, u32[]{:S(2)}, u32[]{:S(2)}) collective-permute-start(bf16[256,1024]{0,1:T(8,128)(2,1)} %copy.107), channel_id=1, source_target_pairs={{28,0},{0,4},{4,8},{8,12},{12,16},{16,20},{20,24},{24,28},{29,1},{... | collective-permute-start | bytes 1572872 | tf_op jit(solution)/shard_map/while/body/eval_jaxpr/ppermute | solution.py:13
  614.1 32.0 %collective-permute-start.2 = (bf16[256,1024]{0,1:T(8,128)(2,1)}, bf16[256,1024]{0,1:T(8,128)(2,1)}, u32[]{:S(2)}, u32[]{:S(2)}) collective-permute-start(bf16[256,1024]{0,1:T(8,128)(2,1)} %fusion.169), channel_id=1, source_target_pairs={{28,0},{0,4},{4,8},{8,12},{12,16},{16,20},{20,24},{24,28},{29,1},{... | collective-permute-start | bytes 1572872 | tf_op jit(solution)/shard_map/while/body/eval_jaxpr/ppermute | solution.py:13
  617.4 35.5 %collective-permute-start.3 = (bf16[256,1024]{0,1:T(8,128)(2,1)}, bf16[256,1024]{0,1:T(8,128)(2,1)}, u32[]{:S(2)}, u32[]{:S(2)}) collective-permute-start(bf16[256,1024]{0,1:T(8,128)(2,1)} %fusion.171), channel_id=1, source_target_pairs={{28,0},{0,4},{4,8},{8,12},{12,16},{16,20},{20,24},{24,28},{29,1},{... | collective-permute-start | bytes 1572872 | tf_op jit(solution)/shard_map/while/body/eval_jaxpr/ppermute | solution.py:13
  618.2 36.9 %copy-start.22 = (bf16[256,1024]{0,1:T(8,128)(2,1)S(1)}, bf16[256,1024]{0,1:T(8,128)(2,1)}, u32[]{:S(2)}) copy-start(bf16[256,1024]{0,1:T(8,128)(2,1)} %copy-done.21) | copy-start | bytes 1572868 | tf_op jit(solution)/shard_map/while
  618.8 36.2 %copy-start.3 = (f32[256,1024]{0,1:T(8,128)}, f32[256,1024]{0,1:T(8,128)S(1)}, u32[]{:S(2)}) copy-start(f32[256,1024]{0,1:T(8,128)S(1)} %bitcast_add_fusion.4) | copy-start | bytes 3145732 | tf_op jit(solution)/shard_map/while
  656.3 48.1 %collective-permute-start = (bf16[256,1024]{0,1:T(8,128)(2,1)S(1)}, bf16[256,1024]{0,1:T(8,128)(2,1)}, u32[]{:S(2)}, u32[]{:S(2)}) collective-permute-start(bf16[256,1024]{0,1:T(8,128)(2,1)S(1)} %copy.106), channel_id=1, source_target_pairs={{28,0},{0,4},{4,8},{8,12},{12,16},{16,20},{20,24},{24,28},{29,1},{... | collective-permute-start | bytes 1572872 | tf_op jit(solution)/shard_map/while/body/eval_jaxpr/ppermute | solution.py:13
  658.2 46.3 %collective-permute-start.1 = (bf16[256,1024]{0,1:T(8,128)(2,1)}, bf16[256,1024]{0,1:T(8,128)(2,1)}, u32[]{:S(2)}, u32[]{:S(2)}) collective-permute-start(bf16[256,1024]{0,1:T(8,128)(2,1)} %copy.107), channel_id=1, source_target_pairs={{28,0},{0,4},{4,8},{8,12},{12,16},{16,20},{20,24},{24,28},{29,1},{... | collective-permute-start | bytes 1572872 | tf_op jit(solution)/shard_map/while/body/eval_jaxpr/ppermute | solution.py:13
  664.4 32.0 %collective-permute-start.2 = (bf16[256,1024]{0,1:T(8,128)(2,1)}, bf16[256,1024]{0,1:T(8,128)(2,1)}, u32[]{:S(2)}, u32[]{:S(2)}) collective-permute-start(bf16[256,1024]{0,1:T(8,128)(2,1)} %fusion.169), channel_id=1, source_target_pairs={{28,0},{0,4},{4,8},{8,12},{12,16},{16,20},{20,24},{24,28},{29,1},{... | collective-permute-start | bytes 1572872 | tf_op jit(solution)/shard_map/while/body/eval_jaxpr/ppermute | solution.py:13
  667.7 34.6 %collective-permute-start.3 = (bf16[256,1024]{0,1:T(8,128)(2,1)}, bf16[256,1024]{0,1:T(8,128)(2,1)}, u32[]{:S(2)}, u32[]{:S(2)}) collective-permute-start(bf16[256,1024]{0,1:T(8,128)(2,1)} %fusion.171), channel_id=1, source_target_pairs={{28,0},{0,4},{4,8},{8,12},{12,16},{16,20},{20,24},{24,28},{29,1},{... | collective-permute-start | bytes 1572872 | tf_op jit(solution)/shard_map/while/body/eval_jaxpr/ppermute | solution.py:13
  668.5 36.0 %copy-start.22 = (bf16[256,1024]{0,1:T(8,128)(2,1)S(1)}, bf16[256,1024]{0,1:T(8,128)(2,1)}, u32[]{:S(2)}) copy-start(bf16[256,1024]{0,1:T(8,128)(2,1)} %copy-done.21) | copy-start | bytes 1572868 | tf_op jit(solution)/shard_map/while
  669.2 35.3 %copy-start.3 = (f32[256,1024]{0,1:T(8,128)}, f32[256,1024]{0,1:T(8,128)S(1)}, u32[]{:S(2)}) copy-start(f32[256,1024]{0,1:T(8,128)S(1)} %bitcast_add_fusion.4) | copy-start | bytes 3145732 | tf_op jit(solution)/shard_map/while
  705.7 47.2 %collective-permute-start = (bf16[256,1024]{0,1:T(8,128)(2,1)S(1)}, bf16[256,1024]{0,1:T(8,128)(2,1)}, u32[]{:S(2)}, u32[]{:S(2)}) collective-permute-start(bf16[256,1024]{0,1:T(8,128)(2,1)S(1)} %copy.106), channel_id=1, source_target_pairs={{28,0},{0,4},{4,8},{8,12},{12,16},{16,20},{20,24},{24,28},{29,1},{... | collective-permute-start | bytes 1572872 | tf_op jit(solution)/shard_map/while/body/eval_jaxpr/ppermute | solution.py:13
  707.6 45.4 %collective-permute-start.1 = (bf16[256,1024]{0,1:T(8,128)(2,1)}, bf16[256,1024]{0,1:T(8,128)(2,1)}, u32[]{:S(2)}, u32[]{:S(2)}) collective-permute-start(bf16[256,1024]{0,1:T(8,128)(2,1)} %copy.107), channel_id=1, source_target_pairs={{28,0},{0,4},{4,8},{8,12},{12,16},{16,20},{20,24},{24,28},{29,1},{... | collective-permute-start | bytes 1572872 | tf_op jit(solution)/shard_map/while/body/eval_jaxpr/ppermute | solution.py:13
  713.8 31.4 %collective-permute-start.2 = (bf16[256,1024]{0,1:T(8,128)(2,1)}, bf16[256,1024]{0,1:T(8,128)(2,1)}, u32[]{:S(2)}, u32[]{:S(2)}) collective-permute-start(bf16[256,1024]{0,1:T(8,128)(2,1)} %fusion.169), channel_id=1, source_target_pairs={{28,0},{0,4},{4,8},{8,12},{12,16},{16,20},{20,24},{24,28},{29,1},{... | collective-permute-start | bytes 1572872 | tf_op jit(solution)/shard_map/while/body/eval_jaxpr/ppermute | solution.py:13
  717.2 33.7 %collective-permute-start.3 = (bf16[256,1024]{0,1:T(8,128)(2,1)}, bf16[256,1024]{0,1:T(8,128)(2,1)}, u32[]{:S(2)}, u32[]{:S(2)}) collective-permute-start(bf16[256,1024]{0,1:T(8,128)(2,1)} %fusion.171), channel_id=1, source_target_pairs={{28,0},{0,4},{4,8},{8,12},{12,16},{16,20},{20,24},{24,28},{29,1},{... | collective-permute-start | bytes 1572872 | tf_op jit(solution)/shard_map/while/body/eval_jaxpr/ppermute | solution.py:13
  717.9 35.0 %copy-start.22 = (bf16[256,1024]{0,1:T(8,128)(2,1)S(1)}, bf16[256,1024]{0,1:T(8,128)(2,1)}, u32[]{:S(2)}) copy-start(bf16[256,1024]{0,1:T(8,128)(2,1)} %copy-done.21) | copy-start | bytes 1572868 | tf_op jit(solution)/shard_map/while
  718.6 34.3 %copy-start.3 = (f32[256,1024]{0,1:T(8,128)}, f32[256,1024]{0,1:T(8,128)S(1)}, u32[]{:S(2)}) copy-start(f32[256,1024]{0,1:T(8,128)S(1)} %bitcast_add_fusion.4) | copy-start | bytes 3145732 | tf_op jit(solution)/shard_map/while
  754.2 46.3 %collective-permute-start = (bf16[256,1024]{0,1:T(8,128)(2,1)S(1)}, bf16[256,1024]{0,1:T(8,128)(2,1)}, u32[]{:S(2)}, u32[]{:S(2)}) collective-permute-start(bf16[256,1024]{0,1:T(8,128)(2,1)S(1)} %copy.106), channel_id=1, source_target_pairs={{28,0},{0,4},{4,8},{8,12},{12,16},{16,20},{20,24},{24,28},{29,1},{... | collective-permute-start | bytes 1572872 | tf_op jit(solution)/shard_map/while/body/eval_jaxpr/ppermute | solution.py:13
  756.1 44.4 %collective-permute-start.1 = (bf16[256,1024]{0,1:T(8,128)(2,1)}, bf16[256,1024]{0,1:T(8,128)(2,1)}, u32[]{:S(2)}, u32[]{:S(2)}) collective-permute-start(bf16[256,1024]{0,1:T(8,128)(2,1)} %copy.107), channel_id=1, source_target_pairs={{28,0},{0,4},{4,8},{8,12},{12,16},{16,20},{20,24},{24,28},{29,1},{... | collective-permute-start | bytes 1572872 | tf_op jit(solution)/shard_map/while/body/eval_jaxpr/ppermute | solution.py:13
  762.3 30.5 %collective-permute-start.2 = (bf16[256,1024]{0,1:T(8,128)(2,1)}, bf16[256,1024]{0,1:T(8,128)(2,1)}, u32[]{:S(2)}, u32[]{:S(2)}) collective-permute-start(bf16[256,1024]{0,1:T(8,128)(2,1)} %fusion.169), channel_id=1, source_target_pairs={{28,0},{0,4},{4,8},{8,12},{12,16},{16,20},{20,24},{24,28},{29,1},{... | collective-permute-start | bytes 1572872 | tf_op jit(solution)/shard_map/while/body/eval_jaxpr/ppermute | solution.py:13
  765.7 32.8 %collective-permute-start.3 = (bf16[256,1024]{0,1:T(8,128)(2,1)}, bf16[256,1024]{0,1:T(8,128)(2,1)}, u32[]{:S(2)}, u32[]{:S(2)}) collective-permute-start(bf16[256,1024]{0,1:T(8,128)(2,1)} %fusion.171), channel_id=1, source_target_pairs={{28,0},{0,4},{4,8},{8,12},{12,16},{16,20},{20,24},{24,28},{29,1},{... | collective-permute-start | bytes 1572872 | tf_op jit(solution)/shard_map/while/body/eval_jaxpr/ppermute | solution.py:13
  804.1 70.5 %reduce-scatter.9.cloned.1.call-start = ((), (), s32[]{:S(2)}) async-start(), calls=%async_computation.15 | async-start | bytes 2621440 | tf_op jit(solution)/shard_map/reduce_scatter | solution.py:108
  806.3 95.1 %reduce-scatter.11.cloned.1.call-start = ((), (), s32[]{:S(2)}) async-start(), calls=%async_computation.16 | async-start | bytes 2621440 | tf_op jit(solution)/shard_map/reduce_scatter | solution.py:108
  808.4 127.0 %reduce-scatter.13.cloned.1.call-start = ((), (), s32[]{:S(2)}) async-start(), calls=%async_computation.17 | async-start | bytes 2621440 | tf_op jit(solution)/shard_map/reduce_scatter | solution.py:108
  812.1 197.6 %reduce-scatter.15.cloned.1.call-start = ((), (), s32[]{:S(2)}) async-start(), calls=%async_computation.18 | async-start | bytes 10485760 | tf_op jit(solution)/shard_map/reduce_scatter | solution.py:108
  819.6 264.5 %reduce-scatter.17.cloned.1.call-start = ((), (), s32[]{:S(2)}) async-start(), calls=%async_computation.19 | async-start | bytes 10485760 | tf_op jit(solution)/shard_map/reduce_scatter | solution.py:108
  (66 other events, 447.6 us)
Sparse Core Ops, SparseCore 0:
  9.6 25.2 all-gather.8
  36.5 22.5 all-gather.14
  60.7 22.5 all-gather.12
  85.8 73.4 all-gather.10
  161.9 71.6 all-gather.16
  235.0 20.8 all-gather.18
  257.4 58.2 all-gather.20
  317.3 58.2 all-gather.22
  804.2 27.9 reduce-scatter.6
  834.8 32.4 reduce-scatter.8
  869.8 31.5 reduce-scatter.10
  903.9 31.3 reduce-scatter.12
  938.0 71.7 reduce-scatter.14
  1012.3 71.7 reduce-scatter.16
where the time goes:
time: 1590 us; the launch traced here: 1580 us
  waiting for transfers between devices  689 us (43%)
  blocking collectives  524 us (33%)
  matrix products  194 us (12%)
  other arithmetic  85.1 us (5%)
  local copies, waits for them, and re-layouts  59 us (4%)
    psum x1, blocking collectives, body(): lax.psum((share_query, share_key, share_value, share_out, share_up, share...  485 us
    ppermute x32, waiting for transfers between devices, from_behind(): return lax.ppermute(block, axis, route)  247 us
    reduce_scatter x6, waiting for transfers between devices, owner_rows(): lax.psum_scatter(lax.dot_general(layer_in, layer_grad, (((0,), (0,)), (()...  209 us
    all_gather x1, waiting for transfers between devices, body(): value_piece = lax.all_gather(values, 'ctx', axis=0, tiled=True)  74.2 us
    all_gather x1, waiting for transfers between devices, body(): key_piece = lax.all_gather(key_rows, 'ctx', axis=0, tiled=True)  73.5 us
    psum x1, blocking collectives, body(): lax.psum((grad_query_b, grad_value_b, grad_output_b, grad_attn_gain, grad...  38.5 us
    dot_general x8, matrix products, online_update(): jnp.einsum('hqk,khd->qhd', exp_scores.astype(jnp.bfloat16), value_rows.re...  37.9 us
    while x120, local copies, waits for them, and re-layouts  34.6 us
  transfers between devices with their start and end apart: 46, of which 26 were waited for; matrix products, arithmetic and copies ran while one was open for 18% of the time, Pallas kernels for 0%

commit v1 on v0

--- a/solution.py
+++ b/solution.py
@@ -179,7 +179,12 @@
         jnp.zeros((H, block_len), jnp.float32),
     )
     key_piece = lax.all_gather(key_rows, "ctx", axis=0, tiled=True)
-    value_piece = lax.all_gather(values, "ctx", axis=0, tiled=True)
+    ring = [values]
+    for hop in range(7):
+        ring.append(lax.ppermute(ring[-1], "ctx", [(dev, (dev + 1) % 8) for dev in range(8)]))
+    value_piece = jnp.roll(
+        jnp.concatenate(ring[::-1], axis=0), (lax.axis_index("ctx") + 1) * ring[0].shape[0], axis=0
+    )
     shards = key_piece.shape[0] // block_len
 
     def one_shard(index, inner):

time: 1590 us -> 1530 us (0.962)
  waiting for transfers between devices: 689 us -> 613 us
    ppermute x0 -> x7, waiting for transfers between devices: none -> 133 us  [body(): lax.ppermute(ring[-1], 'ctx', [(dev, (dev + 1) % 8) for dev in range(8)])]
    all_gather x1 -> x0, waiting for transfers between devices: 74.2 us -> none  [body(): value_piece = lax.all_gather(values, 'ctx', axis=0, tiled=True)]
    all_gather x1, waiting for transfers between devices: 73.5 us -> 0.01 us  [body(): key_piece = lax.all_gather(key_rows, 'ctx', axis=0, tiled=True)]
    reduce_scatter x6, waiting for transfers between devices: 209 us -> 178 us  [owner_rows(): lax.psum_scatter(lax.dot_general(layer_in, layer_grad, (((0,), (0,)), (()...]
  transfers between devices with their start and end apart: 46 -> 52, of which waited for: 26 -> 29; matrix products, arithmetic and copies ran while one was open for 18% -> 21% of each run, Pallas kernels for 0% -> 0%
where the time goes in v1:
time: 1530 us; the launch traced here: 1520 us
  waiting for transfers between devices  613 us (40%)
  blocking collectives  524 us (34%)
  matrix products  195 us (13%)
  other arithmetic  84.8 us (6%)
  local copies, waits for them, and re-layouts  73.9 us (5%)
    psum x1, blocking collectives, body(): lax.psum((share_query, share_key, share_value, share_out, share_up, share...  485 us
    ppermute x32, waiting for transfers between devices, from_behind(): return lax.ppermute(block, axis, route)  247 us
    reduce_scatter x6, waiting for transfers between devices, owner_rows(): lax.psum_scatter(lax.dot_general(layer_in, layer_grad, (((0,), (0,)), (()...  178 us
    ppermute x7, waiting for transfers between devices, body(): lax.ppermute(ring[-1], 'ctx', [(dev, (dev + 1) % 8) for dev in range(8)])  133 us
    psum x1, blocking collectives, body(): lax.psum((grad_query_b, grad_value_b, grad_output_b, grad_attn_gain, grad...  38.7 us
    dot_general x8, matrix products, online_update(): jnp.einsum('hqk,khd->qhd', exp_scores.astype(jnp.bfloat16), value_rows.re...  37.4 us
    while x120, local copies, waits for them, and re-layouts  34.6 us
    dot_general x6, matrix products, dense(): return jnp.dot(left, right, preferred_element_type=jnp.float32)  33.6 us
  transfers between devices with their start and end apart: 52, of which 29 were waited for; matrix products, arithmetic and copies ran while one was open for 21% of the time, Pallas kernels for 0%

profile of v1, /device:TPU:0, one launch (start us, length us, event | category | flops | bytes accessed | tf_op | source)
XLA Modules:
  0.0 1521.6 jit_solution(16552227127725843678)
XLA Ops:
  9.5 25.4 %all-gather.8.cloned.1.call-done = bf16[1024,1024]{1,0:T(8,128)(2,1)} async-done(((bf16[256,1024]{1,0:T(8,128)(2,1)}), bf16[1024,1024]{1,0:T(8,128)(2,1)}) %all-gather.8.cloned.1.call-update) | async-done | bytes 2097168 | tf_op jit(solution)/shard_map/all_gather | solution.py:166
  34.9 3.3 convolution_convert_fusion.4
  39.5 19.6 %all-gather.14.cloned.1.call-done = bf16[1024,1024]{1,0:T(8,128)(2,1)} async-done(((bf16[256,1024]{1,0:T(8,128)(2,1)}), bf16[1024,1024]{1,0:T(8,128)(2,1)}) %all-gather.14.cloned.1.call-update) | async-done | bytes 2097168 | tf_op jit(solution)/shard_map/all_gather | solution.py:167
  62.9 15.3 %collective-permute-done.4 = bf16[256,1024]{1,0:T(8,128)(2,1)S(1)} collective-permute-done((bf16[256,1024]{1,0:T(8,128)(2,1)S(1)}, bf16[256,1024]{1,0:T(8,128)(2,1)S(1)}, u32[]{:S(2)}, u32[]{:S(2)}) %collective-permute-start.4) | collective-permute-done | bytes 524320 | tf_op jit(solution)/shard_map/ppermute | solution.py:184
  78.2 15.9 %collective-permute-done.5 = bf16[256,1024]{1,0:T(8,128)(2,1)S(1)} collective-permute-done((bf16[256,1024]{1,0:T(8,128)(2,1)S(1)}, bf16[256,1024]{1,0:T(8,128)(2,1)S(1)}, u32[]{:S(2)}, u32[]{:S(2)}) %collective-permute-start.5) | collective-permute-done | bytes 524320 | tf_op jit(solution)/shard_map/ppermute | solution.py:184
  94.2 26.4 %collective-permute-done.6 = bf16[256,1024]{1,0:T(8,128)(2,1)S(1)} collective-permute-done((bf16[256,1024]{1,0:T(8,128)(2,1)S(1)}, bf16[256,1024]{1,0:T(8,128)(2,1)S(1)}, u32[]{:S(2)}, u32[]{:S(2)}) %collective-permute-start.6) | collective-permute-done | bytes 524320 | tf_op jit(solution)/shard_map/ppermute | solution.py:184
  121.4 16.9 %collective-permute-done.7 = bf16[256,1024]{1,0:T(8,128)(2,1)} collective-permute-done((bf16[256,1024]{1,0:T(8,128)(2,1)S(1)}, bf16[256,1024]{1,0:T(8,128)(2,1)}, u32[]{:S(2)}, u32[]{:S(2)}) %collective-permute-start.7) | collective-permute-done | bytes 524320 | tf_op jit(solution)/shard_map/ppermute | solution.py:184
  138.4 27.7 %collective-permute-done.8 = bf16[256,1024]{1,0:T(8,128)(2,1)} collective-permute-done((bf16[256,1024]{1,0:T(8,128)(2,1)}, bf16[256,1024]{1,0:T(8,128)(2,1)}, u32[]{:S(2)}, u32[]{:S(2)}) %collective-permute-start.8) | collective-permute-done | bytes 524320 | tf_op jit(solution)/shard_map/ppermute | solution.py:184
  167.2 23.6 %collective-permute-done.9 = bf16[256,1024]{1,0:T(8,128)(2,1)} collective-permute-done((bf16[256,1024]{1,0:T(8,128)(2,1)}, bf16[256,1024]{1,0:T(8,128)(2,1)}, u32[]{:S(2)}, u32[]{:S(2)}) %collective-permute-start.9) | collective-permute-done | bytes 524320 | tf_op jit(solution)/shard_map/ppermute | solution.py:184
  193.2 3.2 fusion.44
  197.6 7.4 collective-permute-done.10
  216.6 103.1 %while.42 = (s32[]{:T(128)}, f32[256,16,64]{0,2,1:T(8,128)}, f32[16,256]{1,0:T(8,128)S(1)}, f32[16,256]{1,0:T(8,128)S(1)}, s32[256]{0:T(256)S(1)}, /*index=5*/s3...) while((s32[]{:T(128)}, f32[256,16,64]{0,2,1:T(8,128)}, ...), condition=%wide.region_6.7_spmd.clone, body=%wide.region_3.6_spmd.clone.sunk | while | flops 282943488 | bytes 20975804 | solution.py:196
  221.4 3.2 fusion.156
  224.8 4.3 fusion.155
  233.7 3.8 fusion.156
  237.7 5.3 fusion.155
  247.6 3.2 fusion.156
  251.0 4.6 fusion.155
  260.1 3.2 fusion.156
  263.6 4.6 fusion.155
  272.7 3.3 fusion.156
  276.2 4.6 fusion.155
  285.4 3.2 fusion.156
  288.8 4.6 fusion.155
  295.2 3.1 fusion.153
  298.4 3.8 fusion.156
  302.4 4.6 fusion.155
  311.5 3.2 fusion.156
  314.9 4.7 fusion.155
  323.8 15.8 %fusion.29 = (bf16[256,4096]{1,0:T(8,128)(2,1)}, f32[256,4096]{1,0:T(8,128)}) fusion(f32[4096]{0:T(1024)S(1)} %copy-done.31, bf16[1024,4096]{1,0:T(8,128)(2,1)} %all-gather.18.cloned.1.call-done, f32[256,1024]{1,0:T(8,128)S(1)} %get-tuple-element.758, f32[1024]{0:T(1024)S(1)} %copy-done.26, f32[1024]{0:T(1024)S(1)} %copy-done.25, ...), kind=kOutput, calls=%fused_computation.46 | convolution fusion | flops 2218000384 | bytes 15755264 | tf_op jit(solution)/shard_map/dot_general | solution.py:17
  339.7 5.7 all-gather.20.cloned.1.call-done
  345.4 6.6 fusion.88
  354.2 4.2 convert_reduce_fusion
  363.6 3.1 convolution_convert_fusion.3
  368.3 407.0 %while.43 = (s32[]{:T(128)}, bf16[256,1024]{0,1:T(8,128)(2,1)}, bf16[256,1024]{0,1:T(8,128)(2,1)}, f32[256,1024]{0,1:T(8,128)}, f32[256,1024]{0,1:T(8,128)}, /*i...) while((s32[]{:T(128)}, bf16[256,1024]{0,1:T(8,128)(2,1)}, ...), condition=%wide.region_16.17_spmd.clone, body=%wide.region_15.16_spmd.clone.sunk | while | flops 686882816 | bytes 68932264 | solution.py:243
  375.5 3.2 multiply_convert_fusion.2
  388.6 21.2 %collective-permute-done.2 = bf16[256,1024]{0,1:T(8,128)(2,1)} collective-permute-done((bf16[256,1024]{0,1:T(8,128)(2,1)}, bf16[256,1024]{0,1:T(8,128)(2,1)}, u32[]{:S(2)}, u32[]{:S(2)}) %collective-permute-start.2) | collective-permute-done | bytes 524320 | tf_op jit(solution)/shard_map/while/body/eval_jaxpr/ppermute | solution.py:13
  411.8 8.5 collective-permute-done.3
  427.7 3.1 multiply_convert_fusion.2
  440.6 23.2 %collective-permute-done.2 = bf16[256,1024]{0,1:T(8,128)(2,1)} collective-permute-done((bf16[256,1024]{0,1:T(8,128)(2,1)}, bf16[256,1024]{0,1:T(8,128)(2,1)}, u32[]{:S(2)}, u32[]{:S(2)}) %collective-permute-start.2) | collective-permute-done | bytes 524320 | tf_op jit(solution)/shard_map/while/body/eval_jaxpr/ppermute | solution.py:13
  465.9 7.6 collective-permute-done.3
  479.7 3.1 multiply_convert_fusion.2
  491.9 25.0 %collective-permute-done.2 = bf16[256,1024]{0,1:T(8,128)(2,1)} collective-permute-done((bf16[256,1024]{0,1:T(8,128)(2,1)}, bf16[256,1024]{0,1:T(8,128)(2,1)}, u32[]{:S(2)}, u32[]{:S(2)}) %collective-permute-start.2) | collective-permute-done | bytes 524320 | tf_op jit(solution)/shard_map/while/body/eval_jaxpr/ppermute | solution.py:13
  519.1 6.7 collective-permute-done.3
  542.4 26.8 %collective-permute-done.2 = bf16[256,1024]{0,1:T(8,128)(2,1)} collective-permute-done((bf16[256,1024]{0,1:T(8,128)(2,1)}, bf16[256,1024]{0,1:T(8,128)(2,1)}, u32[]{:S(2)}, u32[]{:S(2)}) %collective-permute-start.2) | collective-permute-done | bytes 524320 | tf_op jit(solution)/shard_map/while/body/eval_jaxpr/ppermute | solution.py:13
  571.3 5.7 collective-permute-done.3
  583.3 3.1 multiply_convert_fusion.2
  593.3 27.2 %collective-permute-done.2 = bf16[256,1024]{0,1:T(8,128)(2,1)} collective-permute-done((bf16[256,1024]{0,1:T(8,128)(2,1)}, bf16[256,1024]{0,1:T(8,128)(2,1)}, u32[]{:S(2)}, u32[]{:S(2)}) %collective-permute-start.2) | collective-permute-done | bytes 524320 | tf_op jit(solution)/shard_map/while/body/eval_jaxpr/ppermute | solution.py:13
  622.6 4.8 collective-permute-done.3
  643.7 27.2 %collective-permute-done.2 = bf16[256,1024]{0,1:T(8,128)(2,1)} collective-permute-done((bf16[256,1024]{0,1:T(8,128)(2,1)}, bf16[256,1024]{0,1:T(8,128)(2,1)}, u32[]{:S(2)}, u32[]{:S(2)}) %collective-permute-start.2) | collective-permute-done | bytes 524320 | tf_op jit(solution)/shard_map/while/body/eval_jaxpr/ppermute | solution.py:13
  673.1 3.9 collective-permute-done.3
  683.1 3.1 multiply_convert_fusion.2
  693.2 26.7 %collective-permute-done.2 = bf16[256,1024]{0,1:T(8,128)(2,1)} collective-permute-done((bf16[256,1024]{0,1:T(8,128)(2,1)}, bf16[256,1024]{0,1:T(8,128)(2,1)}, u32[]{:S(2)}, u32[]{:S(2)}) %collective-permute-start.2) | collective-permute-done | bytes 524320 | tf_op jit(solution)/shard_map/while/body/eval_jaxpr/ppermute | solution.py:13
  722.0 3.5 collective-permute-done.3
  741.8 25.7 %collective-permute-done.2 = bf16[256,1024]{0,1:T(8,128)(2,1)} collective-permute-done((bf16[256,1024]{0,1:T(8,128)(2,1)}, bf16[256,1024]{0,1:T(8,128)(2,1)}, u32[]{:S(2)}, u32[]{:S(2)}) %collective-permute-start.2) | collective-permute-done | bytes 524320 | tf_op jit(solution)/shard_map/while/body/eval_jaxpr/ppermute | solution.py:13
  769.6 3.5 collective-permute-done.3
  775.3 3.5 convert_bitcast_fusion.2
  783.1 7.3 convolution_convert_fusion
  791.7 7.6 convolution_convert_fusion.1
  800.7 38.7 %all-reduce = (f32[1024]{0:T(1024)}, f32[1024]{0:T(1024)}, f32[1024]{0:T(1024)}, f32[1024]{0:T(1024)}, f32[1024]{0:T(1024)}, /*index=5*/f32[4096]{0:T(1024)}, f32[1024]{0:T(1024)}, f32[1024]{0:T(1024)}, f32[1024]{0:T(1024)}) all-reduce(f32[1024]{0:T(1024)S(1)} %convert_reduce_fusion.5, ...), channel_id=1, replica_groups=mesh['ctx'=8,'fsdp'=4] {'ctx','fsdp'}, use_global_device_ids=true, to_apply=%region_20.21 | all-reduce | flops 12288 | bytes 98304 | tf_op jit(solution)/shard_map/psum | solution.py:272
  846.3 29.4 %reduce-scatter.11.cloned.1.call-done = bf16[256,1024]{0,1:T(8,128)(2,1)} async-done(((bf16[1024,1024]{0,1:T(8,128)(2,1)}), bf16[256,1024]{0,1:T(8,128)(2,1)}) %reduce-scatter.11.cloned.1.call-update) | async-done | bytes 524304 | tf_op jit(solution)/shard_map/reduce_scatter | solution.py:108
  875.8 74.2 %reduce-scatter.17.cloned.1.call-done = bf16[1024,1024]{1,0:T(8,128)(2,1)} async-done(((bf16[4096,1024]{1,0:T(8,128)(2,1)}), bf16[1024,1024]{1,0:T(8,128)(2,1)}) %reduce-scatter.17.cloned.1.call-update) | async-done | bytes 2097168 | tf_op jit(solution)/shard_map/reduce_scatter | solution.py:108
  950.0 74.5 %reduce-scatter.15.cloned.1.call-done = bf16[256,4096]{1,0:T(8,128)(2,1)} async-done(((bf16[1024,4096]{1,0:T(8,128)(2,1)}), bf16[256,4096]{1,0:T(8,128)(2,1)}) %reduce-scatter.15.cloned.1.call-update) | async-done | bytes 2097168 | tf_op jit(solution)/shard_map/reduce_scatter | solution.py:108
  1024.5 485.2 %all-reduce.3 = (f32[256,1024]{0,1:T(8,128)}, f32[256,1024]{0,1:T(8,128)S(1)}, f32[256,1024]{0,1:T(8,128)S(1)}, f32[256,1024]{1,0:T(8,128)}, f32[256,4096]{1,0:T(8,128)}, /*index=5*/f32[1024,1024]{1,0:T(8,128)}) all-reduce(bf16[256,1024]{0,1:T(8,128)(2,1)} %reduce-scatter.7.cloned.1.call-done, ...), channel_id=1, replica_groups=mesh['ctx'=8,'fsdp'=4] {'ctx'}, use_global_device_ids=true, to_apply=%region_18.19 | all-reduce | flops 3145728 | bytes 18874368 | tf_op jit(solution)/shard_map/psum | solution.py:259
  (499 shorter events, 234.2 us)
Async XLA Ops:
  7.2 51.9 %copy-start.11 = (bf16[1,16,16,1024]{3,2,1,0:T(8,128)(2,1)S(1)}, bf16[1,16,16,1024]{3,2,1,0:T(8,128)(2,1)}, u32[]{:S(2)}) copy-start(bf16[1,16,16,1024]{3,2,1,0:T(8,128)(2,1)} %param.23) | copy-start | bytes 1572868
  7.2 51.9 %copy-start.32 = (f32[1024]{0:T(1024)S(1)}, f32[1024]{0:T(1024)}, u32[]{:S(2)}) copy-start(f32[1024]{0:T(1024)} %param.30) | copy-start | bytes 12292
  7.2 27.7 %all-gather.8.cloned.1.call-start = ((), (), s32[]{:S(2)}) async-start(), calls=%async_computation.6 | async-start | bytes 2621440 | tf_op jit(solution)/shard_map/all_gather | solution.py:166
  7.9 51.2 %all-gather.14.cloned.1.call-start = ((), (), s32[]{:S(2)}) async-start(), calls=%async_computation.9 | async-start | bytes 2621440 | tf_op jit(solution)/shard_map/all_gather | solution.py:167
  8.7 184.5 %all-gather.12.cloned.1.call-start = ((), (), s32[]{:S(2)}) async-start(), calls=%async_computation.8 | async-start | bytes 2621440 | tf_op jit(solution)/shard_map/all_gather | solution.py:165
  9.4 207.1 %all-gather.10.cloned.1.call-start = ((), (), s32[]{:S(2)}) async-start(), calls=%async_computation.7 | async-start | bytes 4718592 | tf_op jit(solution)/shard_map/all_gather | solution.py:181
  38.2 282.8 %all-gather.16.cloned.1.call-start = ((), (), s32[]{:S(2)}) async-start(), calls=%async_computation.10 | async-start | bytes 2621440 | tf_op jit(solution)/shard_map/all_gather | solution.py:168
  38.8 127.2 %copy-start.13 = (bf16[1,16,16,1024]{3,2,1,0:T(8,128)(2,1)S(1)}, bf16[1,16,16,1024]{3,2,1,0:T(8,128)(2,1)}, u32[]{:S(2)}) copy-start(bf16[1,16,16,1024]{3,2,1,0:T(8,128)(2,1)} %param.41) | copy-start | bytes 1572868
  38.8 127.2 %copy-start.27 = (f32[1024]{0:T(1024)S(1)}, f32[1024]{0:T(1024)}, u32[]{:S(2)}) copy-start(f32[1024]{0:T(1024)} %param.39) | copy-start | bytes 12292
  38.8 128.1 %copy-start.35 = (s32[1,3]{1,0:T(1,128)S(1)}, s32[1,3]{1,0:T(1,128)}, u32[]{:S(2)}) copy-start(s32[1,3]{1,0:T(1,128)} %param.24) | copy-start | bytes 40
  38.8 128.1 %copy-start.36 = (s32[1,3]{1,0:T(1,128)S(1)}, s32[1,3]{1,0:T(1,128)}, u32[]{:S(2)}) copy-start(s32[1,3]{1,0:T(1,128)} %param.25) | copy-start | bytes 40
  38.9 284.9 %all-gather.18.cloned.1.call-start = ((), (), s32[]{:S(2)}) async-start(), calls=%async_computation.11 | async-start | bytes 10485760 | tf_op jit(solution)/shard_map/all_gather | solution.py:169
  39.4 152.7 %copy-start.22 = (bf16[256,1024]{1,0:T(8,128)(2,1)S(1)}, bf16[256,1024]{1,0:T(8,128)(2,1)}, u32[]{:S(2)}) copy-start(bf16[256,1024]{1,0:T(8,128)(2,1)} %convolution_convert_fusion.4) | copy-start | bytes 1572868
  39.4 153.7 %copy-start.33 = (f32[1024]{0:T(1024)S(1)}, f32[1024]{0:T(1024)}, u32[]{:S(2)}) copy-start(f32[1024]{0:T(1024)} %param.27) | copy-start | bytes 12292
  39.5 305.9 %all-gather.20.cloned.1.call-start = ((), (), s32[]{:S(2)}) async-start(), calls=%async_computation.12 | async-start | bytes 10485760 | tf_op jit(solution)/shard_map/all_gather | solution.py:170
  61.4 16.8 %collective-permute-start.4 = (bf16[256,1024]{1,0:T(8,128)(2,1)S(1)}, bf16[256,1024]{1,0:T(8,128)(2,1)S(1)}, u32[]{:S(2)}, u32[]{:S(2)}) collective-permute-start(bf16[256,1024]{1,0:T(8,128)(2,1)S(1)} %fusion.45), channel_id=1, source_target_pairs={{0,4},{4,8},{8,12},{12,16},{16,20},{20,24},{24,28},{28,0},{1,5},{5... | collective-permute-start | bytes 1572872 | tf_op jit(solution)/shard_map/ppermute | solution.py:184
  78.2 15.9 %collective-permute-start.5 = (bf16[256,1024]{1,0:T(8,128)(2,1)S(1)}, bf16[256,1024]{1,0:T(8,128)(2,1)S(1)}, u32[]{:S(2)}, u32[]{:S(2)}) collective-permute-start(bf16[256,1024]{1,0:T(8,128)(2,1)S(1)} %collective-permute-done.4), channel_id=1, source_target_pairs={{0,4},{4,8},{8,12},{12,16},{16,20},{20,24},{24,28},{28,0},{1,5},{5... | collective-permute-start | bytes 1572872 | tf_op jit(solution)/shard_map/ppermute | solution.py:184
  94.2 26.4 %collective-permute-start.6 = (bf16[256,1024]{1,0:T(8,128)(2,1)S(1)}, bf16[256,1024]{1,0:T(8,128)(2,1)S(1)}, u32[]{:S(2)}, u32[]{:S(2)}) collective-permute-start(bf16[256,1024]{1,0:T(8,128)(2,1)S(1)} %collective-permute-done.5), channel_id=1, source_target_pairs={{0,4},{4,8},{8,12},{12,16},{16,20},{20,24},{24,28},{28,0},{1,5},{5... | collective-permute-start | bytes 1572872 | tf_op jit(solution)/shard_map/ppermute | solution.py:184
  121.4 16.9 %collective-permute-start.7 = (bf16[256,1024]{1,0:T(8,128)(2,1)S(1)}, bf16[256,1024]{1,0:T(8,128)(2,1)}, u32[]{:S(2)}, u32[]{:S(2)}) collective-permute-start(bf16[256,1024]{1,0:T(8,128)(2,1)S(1)} %collective-permute-done.6), channel_id=1, source_target_pairs={{0,4},{4,8},{8,12},{12,16},{16,20},{20,24},{24,28},{28,0},{1,5},{5... | collective-permute-start | bytes 1572872 | tf_op jit(solution)/shard_map/ppermute | solution.py:184
  138.3 27.8 %collective-permute-start.8 = (bf16[256,1024]{1,0:T(8,128)(2,1)}, bf16[256,1024]{1,0:T(8,128)(2,1)}, u32[]{:S(2)}, u32[]{:S(2)}) collective-permute-start(bf16[256,1024]{1,0:T(8,128)(2,1)} %collective-permute-done.7), channel_id=1, source_target_pairs={{0,4},{4,8},{8,12},{12,16},{16,20},{20,24},{24,28},{28,0},{1,5},{5... | collective-permute-start | bytes 1572872 | tf_op jit(solution)/shard_map/ppermute | solution.py:184
  138.3 708.0 %reduce-scatter.13.cloned.1.call-start = ((), (), s32[]{:S(2)}) async-start(), calls=%async_computation.16 | async-start | bytes 2621440 | tf_op jit(solution)/shard_map/reduce_scatter | solution.py:108
  166.0 24.7 %collective-permute-start.9 = (bf16[256,1024]{1,0:T(8,128)(2,1)}, bf16[256,1024]{1,0:T(8,128)(2,1)}, u32[]{:S(2)}, u32[]{:S(2)}) collective-permute-start(bf16[256,1024]{1,0:T(8,128)(2,1)} %collective-permute-done.8), channel_id=1, source_target_pairs={{0,4},{4,8},{8,12},{12,16},{16,20},{20,24},{24,28},{28,0},{1,5},{5... | collective-permute-start | bytes 1572872 | tf_op jit(solution)/shard_map/ppermute | solution.py:184
  190.8 14.2 collective-permute-start.10
  216.6 104.5 %copy-start.28 = (f32[1024]{0:T(1024)S(1)}, f32[1024]{0:T(1024)}, u32[]{:S(2)}) copy-start(f32[1024]{0:T(1024)} %param.32) | copy-start | bytes 12292
  323.5 37.7 %copy-start.7 = (f32[256,1024]{1,0:T(8,128)}, f32[256,1024]{1,0:T(8,128)S(1)}, u32[]{:S(2)}) copy-start(f32[256,1024]{1,0:T(8,128)S(1)} %get-tuple-element.758) | copy-start | bytes 3145732
  368.2 478.1 %reduce-scatter.7.cloned.1.call-start = ((), (), s32[]{:S(2)}) async-start(), calls=%async_computation.13 | async-start | bytes 2621440 | tf_op jit(solution)/shard_map/reduce_scatter | solution.py:108
  369.7 52.7 %collective-permute-start = (bf16[256,1024]{0,1:T(8,128)(2,1)S(1)}, bf16[256,1024]{0,1:T(8,128)(2,1)}, u32[]{:S(2)}, u32[]{:S(2)}) collective-permute-start(bf16[256,1024]{0,1:T(8,128)(2,1)S(1)} %copy.121), channel_id=1, source_target_pairs={{28,0},{0,4},{4,8},{8,12},{12,16},{16,20},{20,24},{24,28},{29,1},{... | collective-permute-start | bytes 1572872 | tf_op jit(solution)/shard_map/while/body/eval_jaxpr/ppermute | solution.py:13
  373.0 49.4 %collective-permute-start.1 = (bf16[256,1024]{0,1:T(8,128)(2,1)}, bf16[256,1024]{0,1:T(8,128)(2,1)}, u32[]{:S(2)}, u32[]{:S(2)}) collective-permute-start(bf16[256,1024]{0,1:T(8,128)(2,1)} %copy.122), channel_id=1, source_target_pairs={{28,0},{0,4},{4,8},{8,12},{12,16},{16,20},{20,24},{24,28},{29,1},{... | collective-permute-start | bytes 1572872 | tf_op jit(solution)/shard_map/while/body/eval_jaxpr/ppermute | solution.py:13
  380.9 28.9 %collective-permute-start.2 = (bf16[256,1024]{0,1:T(8,128)(2,1)}, bf16[256,1024]{0,1:T(8,128)(2,1)}, u32[]{:S(2)}, u32[]{:S(2)}) collective-permute-start(bf16[256,1024]{0,1:T(8,128)(2,1)} %fusion.169), channel_id=1, source_target_pairs={{28,0},{0,4},{4,8},{8,12},{12,16},{16,20},{20,24},{24,28},{29,1},{... | collective-permute-start | bytes 1572872 | tf_op jit(solution)/shard_map/while/body/eval_jaxpr/ppermute | solution.py:13
  385.6 34.7 %collective-permute-start.3 = (bf16[256,1024]{0,1:T(8,128)(2,1)}, bf16[256,1024]{0,1:T(8,128)(2,1)}, u32[]{:S(2)}, u32[]{:S(2)}) collective-permute-start(bf16[256,1024]{0,1:T(8,128)(2,1)} %fusion.171), channel_id=1, source_target_pairs={{28,0},{0,4},{4,8},{8,12},{12,16},{16,20},{20,24},{24,28},{29,1},{... | collective-permute-start | bytes 1572872 | tf_op jit(solution)/shard_map/while/body/eval_jaxpr/ppermute | solution.py:13
  423.7 51.9 %collective-permute-start = (bf16[256,1024]{0,1:T(8,128)(2,1)S(1)}, bf16[256,1024]{0,1:T(8,128)(2,1)}, u32[]{:S(2)}, u32[]{:S(2)}) collective-permute-start(bf16[256,1024]{0,1:T(8,128)(2,1)S(1)} %copy.121), channel_id=1, source_target_pairs={{28,0},{0,4},{4,8},{8,12},{12,16},{16,20},{20,24},{24,28},{29,1},{... | collective-permute-start | bytes 1572872 | tf_op jit(solution)/shard_map/while/body/eval_jaxpr/ppermute | solution.py:13
  425.6 50.0 %collective-permute-start.1 = (bf16[256,1024]{0,1:T(8,128)(2,1)}, bf16[256,1024]{0,1:T(8,128)(2,1)}, u32[]{:S(2)}, u32[]{:S(2)}) collective-permute-start(bf16[256,1024]{0,1:T(8,128)(2,1)} %copy.122), channel_id=1, source_target_pairs={{28,0},{0,4},{4,8},{8,12},{12,16},{16,20},{20,24},{24,28},{29,1},{... | collective-permute-start | bytes 1572872 | tf_op jit(solution)/shard_map/while/body/eval_jaxpr/ppermute | solution.py:13
  432.9 30.9 %collective-permute-start.2 = (bf16[256,1024]{0,1:T(8,128)(2,1)}, bf16[256,1024]{0,1:T(8,128)(2,1)}, u32[]{:S(2)}, u32[]{:S(2)}) collective-permute-start(bf16[256,1024]{0,1:T(8,128)(2,1)} %fusion.169), channel_id=1, source_target_pairs={{28,0},{0,4},{4,8},{8,12},{12,16},{16,20},{20,24},{24,28},{29,1},{... | collective-permute-start | bytes 1572872 | tf_op jit(solution)/shard_map/while/body/eval_jaxpr/ppermute | solution.py:13
  436.8 36.7 %collective-permute-start.3 = (bf16[256,1024]{0,1:T(8,128)(2,1)}, bf16[256,1024]{0,1:T(8,128)(2,1)}, u32[]{:S(2)}, u32[]{:S(2)}) collective-permute-start(bf16[256,1024]{0,1:T(8,128)(2,1)} %fusion.171), channel_id=1, source_target_pairs={{28,0},{0,4},{4,8},{8,12},{12,16},{16,20},{20,24},{24,28},{29,1},{... | collective-permute-start | bytes 1572872 | tf_op jit(solution)/shard_map/while/body/eval_jaxpr/ppermute | solution.py:13
  476.9 51.0 %collective-permute-start = (bf16[256,1024]{0,1:T(8,128)(2,1)S(1)}, bf16[256,1024]{0,1:T(8,128)(2,1)}, u32[]{:S(2)}, u32[]{:S(2)}) collective-permute-start(bf16[256,1024]{0,1:T(8,128)(2,1)S(1)} %copy.121), channel_id=1, source_target_pairs={{28,0},{0,4},{4,8},{8,12},{12,16},{16,20},{20,24},{24,28},{29,1},{... | collective-permute-start | bytes 1572872 | tf_op jit(solution)/shard_map/while/body/eval_jaxpr/ppermute | solution.py:13
  478.7 49.1 %collective-permute-start.1 = (bf16[256,1024]{0,1:T(8,128)(2,1)}, bf16[256,1024]{0,1:T(8,128)(2,1)}, u32[]{:S(2)}, u32[]{:S(2)}) collective-permute-start(bf16[256,1024]{0,1:T(8,128)(2,1)} %copy.122), channel_id=1, source_target_pairs={{28,0},{0,4},{4,8},{8,12},{12,16},{16,20},{20,24},{24,28},{29,1},{... | collective-permute-start | bytes 1572872 | tf_op jit(solution)/shard_map/while/body/eval_jaxpr/ppermute | solution.py:13
  485.0 32.0 %collective-permute-start.2 = (bf16[256,1024]{0,1:T(8,128)(2,1)}, bf16[256,1024]{0,1:T(8,128)(2,1)}, u32[]{:S(2)}, u32[]{:S(2)}) collective-permute-start(bf16[256,1024]{0,1:T(8,128)(2,1)} %fusion.169), channel_id=1, source_target_pairs={{28,0},{0,4},{4,8},{8,12},{12,16},{16,20},{20,24},{24,28},{29,1},{... | collective-permute-start | bytes 1572872 | tf_op jit(solution)/shard_map/while/body/eval_jaxpr/ppermute | solution.py:13
  488.3 37.4 %collective-permute-start.3 = (bf16[256,1024]{0,1:T(8,128)(2,1)}, bf16[256,1024]{0,1:T(8,128)(2,1)}, u32[]{:S(2)}, u32[]{:S(2)}) collective-permute-start(bf16[256,1024]{0,1:T(8,128)(2,1)} %fusion.171), channel_id=1, source_target_pairs={{28,0},{0,4},{4,8},{8,12},{12,16},{16,20},{20,24},{24,28},{29,1},{... | collective-permute-start | bytes 1572872 | tf_op jit(solution)/shard_map/while/body/eval_jaxpr/ppermute | solution.py:13
  529.1 50.0 %collective-permute-start = (bf16[256,1024]{0,1:T(8,128)(2,1)S(1)}, bf16[256,1024]{0,1:T(8,128)(2,1)}, u32[]{:S(2)}, u32[]{:S(2)}) collective-permute-start(bf16[256,1024]{0,1:T(8,128)(2,1)S(1)} %copy.121), channel_id=1, source_target_pairs={{28,0},{0,4},{4,8},{8,12},{12,16},{16,20},{20,24},{24,28},{29,1},{... | collective-permute-start | bytes 1572872 | tf_op jit(solution)/shard_map/while/body/eval_jaxpr/ppermute | solution.py:13
  531.0 48.2 %collective-permute-start.1 = (bf16[256,1024]{0,1:T(8,128)(2,1)}, bf16[256,1024]{0,1:T(8,128)(2,1)}, u32[]{:S(2)}, u32[]{:S(2)}) collective-permute-start(bf16[256,1024]{0,1:T(8,128)(2,1)} %copy.122), channel_id=1, source_target_pairs={{28,0},{0,4},{4,8},{8,12},{12,16},{16,20},{20,24},{24,28},{29,1},{... | collective-permute-start | bytes 1572872 | tf_op jit(solution)/shard_map/while/body/eval_jaxpr/ppermute | solution.py:13
  537.2 32.0 %collective-permute-start.2 = (bf16[256,1024]{0,1:T(8,128)(2,1)}, bf16[256,1024]{0,1:T(8,128)(2,1)}, u32[]{:S(2)}, u32[]{:S(2)}) collective-permute-start(bf16[256,1024]{0,1:T(8,128)(2,1)} %fusion.169), channel_id=1, source_target_pairs={{28,0},{0,4},{4,8},{8,12},{12,16},{16,20},{20,24},{24,28},{29,1},{... | collective-permute-start | bytes 1572872 | tf_op jit(solution)/shard_map/while/body/eval_jaxpr/ppermute | solution.py:13
  540.5 36.5 %collective-permute-start.3 = (bf16[256,1024]{0,1:T(8,128)(2,1)}, bf16[256,1024]{0,1:T(8,128)(2,1)}, u32[]{:S(2)}, u32[]{:S(2)}) collective-permute-start(bf16[256,1024]{0,1:T(8,128)(2,1)} %fusion.171), channel_id=1, source_target_pairs={{28,0},{0,4},{4,8},{8,12},{12,16},{16,20},{20,24},{24,28},{29,1},{... | collective-permute-start | bytes 1572872 | tf_op jit(solution)/shard_map/while/body/eval_jaxpr/ppermute | solution.py:13
  541.7 37.4 %copy-start.21 = (bf16[256,1024]{0,1:T(8,128)(2,1)S(1)}, bf16[256,1024]{0,1:T(8,128)(2,1)}, u32[]{:S(2)}) copy-start(bf16[256,1024]{0,1:T(8,128)(2,1)} %copy-done.20) | copy-start | bytes 1572868 | tf_op jit(solution)/shard_map/while
  580.4 49.1 %collective-permute-start = (bf16[256,1024]{0,1:T(8,128)(2,1)S(1)}, bf16[256,1024]{0,1:T(8,128)(2,1)}, u32[]{:S(2)}, u32[]{:S(2)}) collective-permute-start(bf16[256,1024]{0,1:T(8,128)(2,1)S(1)} %copy.121), channel_id=1, source_target_pairs={{28,0},{0,4},{4,8},{8,12},{12,16},{16,20},{20,24},{24,28},{29,1},{... | collective-permute-start | bytes 1572872 | tf_op jit(solution)/shard_map/while/body/eval_jaxpr/ppermute | solution.py:13
  582.3 47.3 %collective-permute-start.1 = (bf16[256,1024]{0,1:T(8,128)(2,1)}, bf16[256,1024]{0,1:T(8,128)(2,1)}, u32[]{:S(2)}, u32[]{:S(2)}) collective-permute-start(bf16[256,1024]{0,1:T(8,128)(2,1)} %copy.122), channel_id=1, source_target_pairs={{28,0},{0,4},{4,8},{8,12},{12,16},{16,20},{20,24},{24,28},{29,1},{... | collective-permute-start | bytes 1572872 | tf_op jit(solution)/shard_map/while/body/eval_jaxpr/ppermute | solution.py:13
  588.5 32.0 %collective-permute-start.2 = (bf16[256,1024]{0,1:T(8,128)(2,1)}, bf16[256,1024]{0,1:T(8,128)(2,1)}, u32[]{:S(2)}, u32[]{:S(2)}) collective-permute-start(bf16[256,1024]{0,1:T(8,128)(2,1)} %fusion.169), channel_id=1, source_target_pairs={{28,0},{0,4},{4,8},{8,12},{12,16},{16,20},{20,24},{24,28},{29,1},{... | collective-permute-start | bytes 1572872 | tf_op jit(solution)/shard_map/while/body/eval_jaxpr/ppermute | solution.py:13
  591.9 35.6 %collective-permute-start.3 = (bf16[256,1024]{0,1:T(8,128)(2,1)}, bf16[256,1024]{0,1:T(8,128)(2,1)}, u32[]{:S(2)}, u32[]{:S(2)}) collective-permute-start(bf16[256,1024]{0,1:T(8,128)(2,1)} %fusion.171), channel_id=1, source_target_pairs={{28,0},{0,4},{4,8},{8,12},{12,16},{16,20},{20,24},{24,28},{29,1},{... | collective-permute-start | bytes 1572872 | tf_op jit(solution)/shard_map/while/body/eval_jaxpr/ppermute | solution.py:13
  592.6 36.9 %copy-start.21 = (bf16[256,1024]{0,1:T(8,128)(2,1)S(1)}, bf16[256,1024]{0,1:T(8,128)(2,1)}, u32[]{:S(2)}) copy-start(bf16[256,1024]{0,1:T(8,128)(2,1)} %copy-done.20) | copy-start | bytes 1572868 | tf_op jit(solution)/shard_map/while
  630.8 48.2 %collective-permute-start = (bf16[256,1024]{0,1:T(8,128)(2,1)S(1)}, bf16[256,1024]{0,1:T(8,128)(2,1)}, u32[]{:S(2)}, u32[]{:S(2)}) collective-permute-start(bf16[256,1024]{0,1:T(8,128)(2,1)S(1)} %copy.121), channel_id=1, source_target_pairs={{28,0},{0,4},{4,8},{8,12},{12,16},{16,20},{20,24},{24,28},{29,1},{... | collective-permute-start | bytes 1572872 | tf_op jit(solution)/shard_map/while/body/eval_jaxpr/ppermute | solution.py:13
  632.7 46.3 %collective-permute-start.1 = (bf16[256,1024]{0,1:T(8,128)(2,1)}, bf16[256,1024]{0,1:T(8,128)(2,1)}, u32[]{:S(2)}, u32[]{:S(2)}) collective-permute-start(bf16[256,1024]{0,1:T(8,128)(2,1)} %copy.122), channel_id=1, source_target_pairs={{28,0},{0,4},{4,8},{8,12},{12,16},{16,20},{20,24},{24,28},{29,1},{... | collective-permute-start | bytes 1572872 | tf_op jit(solution)/shard_map/while/body/eval_jaxpr/ppermute | solution.py:13
  638.9 32.0 %collective-permute-start.2 = (bf16[256,1024]{0,1:T(8,128)(2,1)}, bf16[256,1024]{0,1:T(8,128)(2,1)}, u32[]{:S(2)}, u32[]{:S(2)}) collective-permute-start(bf16[256,1024]{0,1:T(8,128)(2,1)} %fusion.169), channel_id=1, source_target_pairs={{28,0},{0,4},{4,8},{8,12},{12,16},{16,20},{20,24},{24,28},{29,1},{... | collective-permute-start | bytes 1572872 | tf_op jit(solution)/shard_map/while/body/eval_jaxpr/ppermute | solution.py:13
  642.3 34.7 %collective-permute-start.3 = (bf16[256,1024]{0,1:T(8,128)(2,1)}, bf16[256,1024]{0,1:T(8,128)(2,1)}, u32[]{:S(2)}, u32[]{:S(2)}) collective-permute-start(bf16[256,1024]{0,1:T(8,128)(2,1)} %fusion.171), channel_id=1, source_target_pairs={{28,0},{0,4},{4,8},{8,12},{12,16},{16,20},{20,24},{24,28},{29,1},{... | collective-permute-start | bytes 1572872 | tf_op jit(solution)/shard_map/while/body/eval_jaxpr/ppermute | solution.py:13
  680.3 47.3 %collective-permute-start = (bf16[256,1024]{0,1:T(8,128)(2,1)S(1)}, bf16[256,1024]{0,1:T(8,128)(2,1)}, u32[]{:S(2)}, u32[]{:S(2)}) collective-permute-start(bf16[256,1024]{0,1:T(8,128)(2,1)S(1)} %copy.121), channel_id=1, source_target_pairs={{28,0},{0,4},{4,8},{8,12},{12,16},{16,20},{20,24},{24,28},{29,1},{... | collective-permute-start | bytes 1572872 | tf_op jit(solution)/shard_map/while/body/eval_jaxpr/ppermute | solution.py:13
  682.2 45.4 %collective-permute-start.1 = (bf16[256,1024]{0,1:T(8,128)(2,1)}, bf16[256,1024]{0,1:T(8,128)(2,1)}, u32[]{:S(2)}, u32[]{:S(2)}) collective-permute-start(bf16[256,1024]{0,1:T(8,128)(2,1)} %copy.122), channel_id=1, source_target_pairs={{28,0},{0,4},{4,8},{8,12},{12,16},{16,20},{20,24},{24,28},{29,1},{... | collective-permute-start | bytes 1572872 | tf_op jit(solution)/shard_map/while/body/eval_jaxpr/ppermute | solution.py:13
  688.4 31.5 %collective-permute-start.2 = (bf16[256,1024]{0,1:T(8,128)(2,1)}, bf16[256,1024]{0,1:T(8,128)(2,1)}, u32[]{:S(2)}, u32[]{:S(2)}) collective-permute-start(bf16[256,1024]{0,1:T(8,128)(2,1)} %fusion.169), channel_id=1, source_target_pairs={{28,0},{0,4},{4,8},{8,12},{12,16},{16,20},{20,24},{24,28},{29,1},{... | collective-permute-start | bytes 1572872 | tf_op jit(solution)/shard_map/while/body/eval_jaxpr/ppermute | solution.py:13
  691.8 33.7 %collective-permute-start.3 = (bf16[256,1024]{0,1:T(8,128)(2,1)}, bf16[256,1024]{0,1:T(8,128)(2,1)}, u32[]{:S(2)}, u32[]{:S(2)}) collective-permute-start(bf16[256,1024]{0,1:T(8,128)(2,1)} %fusion.171), channel_id=1, source_target_pairs={{28,0},{0,4},{4,8},{8,12},{12,16},{16,20},{20,24},{24,28},{29,1},{... | collective-permute-start | bytes 1572872 | tf_op jit(solution)/shard_map/while/body/eval_jaxpr/ppermute | solution.py:13
  728.9 46.4 %collective-permute-start = (bf16[256,1024]{0,1:T(8,128)(2,1)S(1)}, bf16[256,1024]{0,1:T(8,128)(2,1)}, u32[]{:S(2)}, u32[]{:S(2)}) collective-permute-start(bf16[256,1024]{0,1:T(8,128)(2,1)S(1)} %copy.121), channel_id=1, source_target_pairs={{28,0},{0,4},{4,8},{8,12},{12,16},{16,20},{20,24},{24,28},{29,1},{... | collective-permute-start | bytes 1572872 | tf_op jit(solution)/shard_map/while/body/eval_jaxpr/ppermute | solution.py:13
  730.7 44.5 %collective-permute-start.1 = (bf16[256,1024]{0,1:T(8,128)(2,1)}, bf16[256,1024]{0,1:T(8,128)(2,1)}, u32[]{:S(2)}, u32[]{:S(2)}) collective-permute-start(bf16[256,1024]{0,1:T(8,128)(2,1)} %copy.122), channel_id=1, source_target_pairs={{28,0},{0,4},{4,8},{8,12},{12,16},{16,20},{20,24},{24,28},{29,1},{... | collective-permute-start | bytes 1572872 | tf_op jit(solution)/shard_map/while/body/eval_jaxpr/ppermute | solution.py:13
  737.0 30.5 %collective-permute-start.2 = (bf16[256,1024]{0,1:T(8,128)(2,1)}, bf16[256,1024]{0,1:T(8,128)(2,1)}, u32[]{:S(2)}, u32[]{:S(2)}) collective-permute-start(bf16[256,1024]{0,1:T(8,128)(2,1)} %fusion.169), channel_id=1, source_target_pairs={{28,0},{0,4},{4,8},{8,12},{12,16},{16,20},{20,24},{24,28},{29,1},{... | collective-permute-start | bytes 1572872 | tf_op jit(solution)/shard_map/while/body/eval_jaxpr/ppermute | solution.py:13
  740.3 32.8 %collective-permute-start.3 = (bf16[256,1024]{0,1:T(8,128)(2,1)}, bf16[256,1024]{0,1:T(8,128)(2,1)}, u32[]{:S(2)}, u32[]{:S(2)}) collective-permute-start(bf16[256,1024]{0,1:T(8,128)(2,1)} %fusion.171), channel_id=1, source_target_pairs={{28,0},{0,4},{4,8},{8,12},{12,16},{16,20},{20,24},{24,28},{29,1},{... | collective-permute-start | bytes 1572872 | tf_op jit(solution)/shard_map/while/body/eval_jaxpr/ppermute | solution.py:13
  778.8 67.5 %reduce-scatter.9.cloned.1.call-start = ((), (), s32[]{:S(2)}) async-start(), calls=%async_computation.14 | async-start | bytes 2621440 | tf_op jit(solution)/shard_map/reduce_scatter | solution.py:108
  781.0 94.8 %reduce-scatter.11.cloned.1.call-start = ((), (), s32[]{:S(2)}) async-start(), calls=%async_computation.15 | async-start | bytes 2621440 | tf_op jit(solution)/shard_map/reduce_scatter | solution.py:108
  783.1 166.9 %reduce-scatter.17.cloned.1.call-start = ((), (), s32[]{:S(2)}) async-start(), calls=%async_computation.18 | async-start | bytes 10485760 | tf_op jit(solution)/shard_map/reduce_scatter | solution.py:108
  790.5 234.0 %reduce-scatter.15.cloned.1.call-start = ((), (), s32[]{:S(2)}) async-start(), calls=%async_computation.17 | async-start | bytes 10485760 | tf_op jit(solution)/shard_map/reduce_scatter | solution.py:108
  (72 other events, 711.0 us)
Sparse Core Ops, SparseCore 0:
  9.6 25.2 all-gather.7
  36.5 22.5 all-gather.13
  60.7 22.5 all-gather.11
  85.8 100.8 all-gather.9
  188.1 37.5 all-gather.15
  227.2 58.3 all-gather.17
  287.1 58.2 all-gather.19
  368.4 31.4 reduce-scatter.12
  778.9 27.8 reduce-scatter.6
  809.2 32.3 reduce-scatter.8
  844.3 31.4 reduce-scatter.10
  878.2 71.7 reduce-scatter.16
  952.8 71.6 reduce-scatter.14
